TPU v7x, 32 devices: a whole 2x2x4 slice. The times are simulated.
32 devices in a mesh: dp: 2 (over x), pipe: 2 (over core), ctx: 8 (over z, y).
Axes of the slice: x: 2, y: 2, z: 4, core: 2. Of those that a mesh axis runs over, the one named last changes fastest.
Arguments:
- section_input: bfloat16 [2, 2, 1024, 2048], P('dp', 'pipe', 'ctx'), may hold values from -6 to 6
- section_positions: int32 [2, 2, 1024], P('dp', 'pipe', 'ctx'), may hold values from 0 to 1023, as said below
- saved_input: bfloat16 [2, 2, 1024, 2048], P('dp', 'pipe', 'ctx'), may hold values from -6 to 6
- saved_positions: int32 [2, 2, 1024], P('dp', 'pipe', 'ctx'), may hold values from 0 to 1023, as said below
- cotangent: bfloat16 [2, 2, 1024, 2048], P('dp', 'pipe', 'ctx'), may hold values from -6 to 6
- norm_gains: float32 [2, 2, 2, 2048], P(None, 'pipe'), may hold values from -2 to 2
- output_gains: float32 [2, 2, 2048], P(None, 'pipe'), may hold values from 0.25 to 2
- plan: int32 [2, 2, 2], P('dp', 'pipe'), may hold values from 0 to 1
Outputs:
- next_input: bfloat16 [2, 2, 1024, 2048], P('dp', 'pipe', 'ctx')
- upstream_grad: bfloat16 [2, 2, 1024, 2048], P('dp', 'pipe', 'ctx')
- gain_grads: float32 [2, 3, 2048], P('pipe')
Inputs may be any that keep to these rules, and one draw needn't show every extreme that they name: `section_positions`: in every sequence the first position is 0 and each later one is either one more than the position before it or 0 (a new document). `saved_positions`: in every sequence the first position is 0 and each later one is either one more than the position before it or 0 (a new document).
All inputs are finite; a program needn't handle non-finite values.
Results may differ from a plain program's by a relative error of at most 0.0075.
Values may be sent and summed in bfloat16 or wider, within the bound.
A program may use at most 64 MiB of HBM per device.

v0:
```python
import functools

import jax
import jax.numpy as jnp
from jax import lax
from jax.experimental import pallas as pl
from jax.experimental.pallas import tpu as pltpu
from jax.sharding import PartitionSpec as P

HEADS = 16
HEAD_DIM = 128
FEATURES = 2048
WINDOW = 512
TOK = 128
REACH = WINDOW // TOK
SPAN = WINDOW + TOK
CHUNKS = 4
WIDTH = FEATURES // CHUNKS
CHUNK_HEADS = HEADS // CHUNKS
EPSILON = 1e-06
SCALE = HEAD_DIM**-0.5
MESH = pl.DeviceIdType.MESH
F32 = jnp.float32
BF16 = jnp.bfloat16
A, B, C, D = range(4)
LAST = CHUNKS - 1


def sum_stages(sizes):
    stages = []
    for axis in ("dp", "ctx"):
        left, stride = sizes[axis], 1
        while left > 1:
            factor = next(f for f in range(2, left + 1) if left % f == 0)
            stages.append((axis, stride, factor))
            left //= factor
            stride *= factor
    return stages


def slot(reach):
    return (REACH - reach) * TOK


def dot(left, right, left_dim, right_dim):
    return lax.dot_general(
        left, right, (((left_dim,), (right_dim,)), ((), ())), preferred_element_type=F32
    )


def kernel(
    sizes,
    sec_ref,
    sec_pos,
    sav_ref,
    sav_pos,
    cot_ref,
    norm_ref,
    outg_ref,
    plan_ref,
    next_ref,
    up_ref,
    total_ref,
    keys,
    cot,
    gains,
    masks,
    grads,
    own,
    from_partner,
    from_z3,
    from_z4,
    from_z2,
    produced,
    dx,
    sums,
    load_sem,
    key_send,
    key_recv,
    grad_send,
    grad_recv,
    out_send,
    out_recv,
    sum_send,
    sum_recv,
):
    n = sizes["ctx"]
    c = lax.axis_index("ctx")
    odd = lax.rem(c, 2)
    even = odd == 0
    partner = c + 1 - 2 * odd
    pipe = lax.axis_index("pipe")
    after = lax.rem(pipe + 1, sizes["pipe"])
    before = lax.rem(pipe + sizes["pipe"] - 1, sizes["pipe"])
    up, down = c + 2 < n, c >= 2
    stages = sum_stages(sizes)

    def rows(first):
        if isinstance(first, int):
            return pl.ds(first, TOK)
        return pl.ds(pl.multiple_of(first, TOK), TOK)

    def columns(j):
        return pl.ds(pl.multiple_of(j * WIDTH, WIDTH), WIDTH)

    def load(which, j):
        source = (sav_ref, sec_ref, cot_ref)[which]
        target = cot.at[j] if which == 2 else keys.at[which, j, rows(WINDOW)]
        return pltpu.make_async_copy(source.at[:, columns(j)], target, load_sem.at[which, j])

    def key_copy(t, kind, j):
        if kind == A:
            source, target, device = slot(0), slot(2), c + 2
        elif kind == B:
            source, target, device = slot(2), slot(4), c + 2
        elif kind == C:
            source, target, device = jnp.where(even, slot(0), slot(2)), slot(1), partner
        else:
            source = jnp.where(j == LAST, slot(1), jnp.where(even, slot(2), slot(4)))
            target, device = slot(3), jnp.where(j == LAST, c + 2, partner)
        return pltpu.make_async_remote_copy(
            src_ref=keys.at[t, j, rows(source)],
            dst_ref=keys.at[t, j, rows(target)],
            send_sem=key_send.at[t, kind, j],
            recv_sem=key_recv.at[t, kind, j],
            device_id={"ctx": device},
            device_id_type=MESH,
        )

    def sends_key(kind, j):
        if kind == D:
            return ((j == LAST) & up & (c >= 1)) | ((j < LAST) & (c >= 2 + 2 * odd))
        return (up, up & down, even | down)[kind]

    gets_key = (c >= 2, c >= 4, c >= 1, c >= 3)

    def grad_copy(kind, j):
        first = slot((3, 4, 1, 2)[kind])
        target = (from_z3, from_z4, from_partner, from_z2)[kind].at[j]
        return pltpu.make_async_remote_copy(
            src_ref=grads.at[j, rows(first)],
            dst_ref=target,
            send_sem=grad_send.at[kind, j],
            recv_sem=grad_recv.at[kind, j],
            device_id={"ctx": partner if kind == 2 else c - 2},
            device_id_type=MESH,
        )

    sends_grad = (down, down, None, down)

    def out_copy(kind, j):
        return pltpu.make_async_remote_copy(
            src_ref=(produced, dx)[kind].at[j],
            dst_ref=(next_ref, up_ref)[kind].at[:, columns(j)],
            send_sem=out_send.at[kind, j],
            recv_sem=out_recv.at[kind, j],
            device_id={"pipe": (after, before)[kind]},
            device_id_type=MESH,
        )

    def digit_of(stage):
        axis, stride, factor = stages[stage]
        return lax.rem(lax.axis_index(axis) // stride, factor)

    def sum_peer(stage, offset):
        axis, stride, factor = stages[stage]
        digit = digit_of(stage)
        return {axis: lax.axis_index(axis) + (lax.rem(digit + offset, factor) - digit) * stride}

    def sum_copy(stage, offset, sender):
        return pltpu.make_async_remote_copy(
            src_ref=sums.at[stage, digit_of(stage)],
            dst_ref=sums.at[stage, sender],
            send_sem=sum_send.at[stage, offset - 1],
            recv_sem=sum_recv.at[stage, offset - 1],
            device_id=sum_peer(stage, offset),
            device_id_type=MESH,
        )

    def start_sum(stage):
        for offset in range(1, stages[stage][2]):
            sum_copy(stage, offset, digit_of(stage)).start()

    def finish_sum(stage):
        factor = stages[stage][2]
        for offset in range(1, factor):
            sender = lax.rem(digit_of(stage) + factor - offset, factor)
            sum_copy(stage, offset, sender).wait_recv()
        total = sums[stage, 0]
        for digit in range(1, factor):
            total = total + sums[stage, digit]
        if stage + 1 < len(stages):
            sums[stage + 1, digit_of(stage + 1)] = total
            start_sum(stage + 1)
        else:
            total_ref[...] = total * (1.0 / TOK)

    def when(condition, action):
        if condition is None:
            action()
        else:
            pl.when(condition)(action)

    def start_key(t, kind, j, extra=None):
        condition = sends_key(kind, j)
        if extra is not None:
            condition = condition & extra
        when(condition, lambda: key_copy(t, kind, j).start())

    def wait_key(t, kind, j, extra=None):
        condition = gets_key[kind]
        if extra is not None:
            condition = condition & extra
        when(condition, lambda: key_copy(t, kind, j).wait_recv())

    def each(action):
        @pl.loop(0, CHUNKS)
        def _(j):
            action(j)

    each(lambda j: load(0, j).start())
    barrier = pltpu.get_barrier_semaphore()

    def greet(device):
        pl.semaphore_signal(barrier, inc=1, device_id=device, device_id_type=MESH)

    greet({"ctx": partner})
    greet({"pipe": after})
    count = 2
    if sizes["pipe"] > 2:
        greet({"pipe": before})
        count += 1
    pl.when(up)(lambda: greet({"ctx": c + 2}))
    pl.when(down)(lambda: greet({"ctx": c - 2}))
    for stage, (axis, stride, factor) in enumerate(stages):
        if axis == "ctx" and factor == 2 and stride <= 2:
            continue
        for offset in range(1, factor):
            greet(sum_peer(stage, offset))
            count += 1
    each(lambda j: load(1, j).start())
    each(lambda j: load(2, j).start())
    pl.semaphore_wait(barrier, count + up.astype(jnp.int32) + down.astype(jnp.int32))

    def first_saved(j):
        load(0, j).wait()
        start_key(0, A, j)
        start_key(0, C, j, even)

    each(first_saved)

    for which in range(2):
        lap = plan_ref[0, which]
        gains[pl.ds(3 * which, 2), :] = jnp.where(lap == 1, norm_ref[1], norm_ref[0])
        gains[pl.ds(3 * which + 2, 1), :] = jnp.where(lap == 1, outg_ref[1], outg_ref[0])
    distance = (
        lax.broadcasted_iota(jnp.int32, (SPAN, TOK), 1)
        + WINDOW
        - lax.broadcasted_iota(jnp.int32, (SPAN, TOK), 0)
    )
    for t, positions in ((0, sav_pos), (1, sec_pos)):
        allowed = (distance >= 0) & (distance < WINDOW) & (distance <= positions[...])
        masks[t] = jnp.where(allowed, 1.0, 0.0).astype(F32)
    for reach in range(1, REACH + 1):

        @pl.when(c < reach)
        def _():
            @pl.loop(0, CHUNKS)
            def _(j):
                for t in range(2):
                    keys[t, j, rows(slot(reach))] = jnp.zeros((TOK, WIDTH), BF16)

    def relay(t, j):
        wait_key(t, A, j)
        start_key(t, B, j)
        start_key(t, C, j, odd == 1)
        start_key(t, D, j, even & (j < LAST))

    def relay_last(t, j):
        wait_key(t, B, j)
        wait_key(t, C, j, j == LAST)
        start_key(t, D, j, (odd == 1) | (j == LAST))

    each(lambda j: relay(0, j))

    def second(j):
        relay_last(0, j)
        load(1, j).wait()
        start_key(1, A, j)
        start_key(1, C, j, even)

    each(second)

    def normed(x):
        wide = x.astype(F32)
        inverse = lax.rsqrt(jnp.mean(wide * wide, axis=-1, keepdims=True) + EPSILON)
        return wide * inverse, inverse

    def lanes_of(h):
        return pl.ds(pl.multiple_of(h * HEAD_DIM, HEAD_DIM), HEAD_DIM)

    def weights(t, n_all, a, b):
        k = (n_all * b).astype(BF16)
        q = (n_all[WINDOW:] * a).astype(BF16)
        w = jnp.exp(dot(k, q, 1, 1) * SCALE) * masks[t]
        prob = w * (1.0 / jnp.sum(w, axis=0, keepdims=True))
        return q, k, prob

    sum_slot = digit_of(0)

    def backward(j):
        @pl.loop(0, CHUNK_HEADS, unroll=4)
        def _(i):
            lanes = lanes_of(i)
            head = j * CHUNK_HEADS + i
            wide = lanes_of(head)
            a, b, g = (gains[pl.ds(3 + m, 1), wide] for m in range(3))
            x = keys[0, j, :, lanes]
            n_all, inverse = normed(x)
            q, k, prob = weights(0, n_all, a, b)
            p = prob.astype(BF16)
            ct = cot[j, :, lanes].astype(F32)
            d_mix = (ct * g).astype(BF16)
            d_prob = dot(x, d_mix, 1, 1)
            delta = jnp.sum(prob * d_prob, axis=0, keepdims=True)
            d_score = (prob * (d_prob - delta)).astype(BF16)
            mix = dot(p, x, 0, 0)
            d_k = dot(d_score, q, 1, 0)
            d_q = dot(d_score, k, 0, 0)
            d_value = dot(p, d_mix, 1, 0)
            n_own = n_all[WINDOW:]
            d_n = d_k * (b * SCALE)
            d_n_own = d_n[WINDOW:] + d_q * (a * SCALE)

            def through_norm(d, value, scale):
                return scale * (d - value * jnp.mean(d * value, axis=-1, keepdims=True))

            grads[j, :, lanes] = (
                d_value[:WINDOW] + through_norm(d_n[:WINDOW], n_all[:WINDOW], inverse[:WINDOW])
            ).astype(BF16)
            own[j, :, lanes] = d_value[WINDOW:] + through_norm(d_n_own, n_own, inverse[WINDOW:]) + ct
            parts = (
                jnp.sum(d_q * n_own, axis=0, keepdims=True) * SCALE,
                jnp.sum(d_k * n_all, axis=0, keepdims=True) * SCALE,
                jnp.sum(ct * mix, axis=0, keepdims=True),
            )
            for m in range(3):
                sums[0, sum_slot, pl.ds(m * HEADS + head, 1), :] = parts[m]

    def forward(j):
        @pl.loop(0, CHUNK_HEADS, unroll=4)
        def _(i):
            lanes = lanes_of(i)
            wide = lanes_of(j * CHUNK_HEADS + i)
            a, b, g = (gains[pl.ds(m, 1), wide] for m in range(3))
            x = keys[1, j, :, lanes]
            n_all, _ = normed(x)
            _, _, prob = weights(1, n_all, a, b)
            mix = dot(prob.astype(BF16), x, 0, 0)
            produced[j, :, lanes] = (x[WINDOW:].astype(F32) + g * mix).astype(BF16)

    def add_to(reach, j, received):
        total = grads[j, rows(slot(reach))].astype(F32) + received[j].astype(F32)
        grads[j, rows(slot(reach))] = total.astype(BF16)

    def merge(j):
        @pl.when(up)
        def _():
            grad_copy(0, j).wait_recv()
            add_to(1, j, from_z3)

        grad_copy(2, j).start()

        @pl.when(up)
        def _():
            grad_copy(1, j).wait_recv()
            add_to(2, j, from_z4)

        pl.when(even & down)(lambda: grad_copy(3, j).start())

    def pass_on(j):
        @pl.when(odd == 1)
        def _():
            grad_copy(2, j).wait_recv()
            add_to(2, j, from_partner)
            pl.when(down)(lambda: grad_copy(3, j).start())

    def send_dx(j):
        @pl.when(even)
        def _():
            grad_copy(2, j).wait_recv()
            own[j] = own[j] + from_partner[j].astype(F32)

        @pl.when(up)
        def _():
            grad_copy(3, j).wait_recv()
            own[j] = own[j] + from_z2[j].astype(F32)

        dx[j] = own[j].astype(BF16)
        out_copy(1, j).start()

    def middle(j):
        wait_key(0, C, j, j < LAST)
        wait_key(0, D, j)
        pl.when(j == 0)(lambda: each(lambda i: load(2, i).wait()))
        backward(j)
        for kind in range(2):
            when(sends_grad[kind], lambda: grad_copy(kind, j).start())
        relay(1, j)
        pl.when(j > 0)(lambda: merge(jnp.maximum(j - 1, 0)))

    each(middle)
    if stages:
        start_sum(0)
    merge(LAST)

    def between(j):
        pass_on(j)
        relay_last(1, j)

    each(between)
    if stages:
        finish_sum(0)

    def last(j):
        wait_key(1, C, j, j < LAST)
        wait_key(1, D, j)
        forward(j)
        out_copy(0, j).start()
        for stage in range(1, min(CHUNKS + 1, len(stages))):
            pl.when(j == stage - 1)(lambda: finish_sum(stage))
        send_dx(j)

    each(last)
    for stage in range(CHUNKS + 1, len(stages)):
        finish_sum(stage)

    def drain(j):
        for t in range(2):
            for kind in range(4):
                when(sends_key(kind, j), lambda: key_copy(t, kind, j).wait_send())
        for kind in range(4):
            when(sends_grad[kind], lambda: grad_copy(kind, j).wait_send())
        for kind in range(2):
            out_copy(kind, j).wait_send()
            out_copy(kind, j).wait_recv()

    each(drain)
    for stage, (_, _, factor) in enumerate(stages):
        for offset in range(1, factor):
            sum_copy(stage, offset, digit_of(stage)).wait_send()


def local(
    sizes,
    section_input,
    section_positions,
    saved_input,
    saved_positions,
    cotangent,
    norm_gains,
    output_gains,
    plan,
):
    stages = sum_stages(sizes)
    widest = max([factor for _, _, factor in stages] + [2])
    depth = max(len(stages), 1)
    in_hbm = pl.BlockSpec(memory_space=pl.ANY)
    in_vmem = pl.BlockSpec(memory_space=pltpu.VMEM)
    block = (CHUNKS, TOK, WIDTH)
    produced, grads, totals = pl.pallas_call(
        functools.partial(kernel, sizes),
        out_shape=(
            jax.ShapeDtypeStruct((TOK, FEATURES), BF16),
            jax.ShapeDtypeStruct((TOK, FEATURES), BF16),
            jax.ShapeDtypeStruct((3 * HEADS, HEAD_DIM), F32),
        ),
        in_specs=[
            in_hbm,
            in_vmem,
            in_hbm,
            in_vmem,
            in_hbm,
            in_vmem,
            in_vmem,
            pl.BlockSpec(memory_space=pltpu.SMEM),
        ],
        out_specs=(in_hbm, in_hbm, in_vmem),
        scratch_shapes=[
            pltpu.VMEM((2, CHUNKS, SPAN, WIDTH), BF16),
            pltpu.VMEM(block, BF16),
            pltpu.VMEM((8, FEATURES), F32),
            pltpu.VMEM((2, SPAN, TOK), F32),
            pltpu.VMEM((CHUNKS, WINDOW, WIDTH), BF16),
            pltpu.VMEM(block, F32),
            pltpu.VMEM(block, BF16),
            pltpu.VMEM(block, BF16),
            pltpu.VMEM(block, BF16),
            pltpu.VMEM(block, BF16),
            pltpu.VMEM(block, BF16),
            pltpu.VMEM(block, BF16),
            pltpu.VMEM((depth, widest, 3 * HEADS, HEAD_DIM), F32),
            pltpu.SemaphoreType.DMA((3, CHUNKS)),
            pltpu.SemaphoreType.DMA((2, 4, CHUNKS)),
            pltpu.SemaphoreType.DMA((2, 4, CHUNKS)),
            pltpu.SemaphoreType.DMA((4, CHUNKS)),
            pltpu.SemaphoreType.DMA((4, CHUNKS)),
            pltpu.SemaphoreType.DMA((2, CHUNKS)),
            pltpu.SemaphoreType.DMA((2, CHUNKS)),
            pltpu.SemaphoreType.DMA((depth, widest)),
            pltpu.SemaphoreType.DMA((depth, widest)),
        ],
        compiler_params=pltpu.CompilerParams(
            collective_id=0, has_side_effects=True, vmem_limit_bytes=60 * 1024 * 1024
        ),
        cost_estimate=pl.CostEstimate(
            flops=9 * 2 * TOK * SPAN * FEATURES,
            bytes_accessed=5 * TOK * FEATURES * 2,
            transcendentals=2 * HEADS * TOK * SPAN,
        ),
    )(
        section_input[0, 0],
        section_positions[0],
        saved_input[0, 0],
        saved_positions[0],
        cotangent[0, 0],
        norm_gains[:, 0],
        output_gains,
        plan[0],
    )
    return (produced[None, None], grads[None, None], totals.reshape(1, 3, FEATURES))


def solution(mesh):
    placed = (
        P("dp", "pipe", "ctx", None),
        P("dp", "pipe", "ctx"),
        P("dp", "pipe", "ctx", None),
        P("dp", "pipe", "ctx"),
        P("dp", "pipe", "ctx", None),
        P(None, "pipe", None, None),
        P(None, "pipe", None),
        P("dp", "pipe", None),
    )
    return jax.shard_map(
        functools.partial(local, {axis: mesh.shape[axis] for axis in ("dp", "pipe", "ctx")}),
        mesh=mesh,
        in_specs=placed,
        out_specs=(
            P("dp", "pipe", "ctx", None),
            P("dp", "pipe", "ctx", None),
            P("pipe", None, None),
        ),
        check_vma=False,
    )
```

profile of v0, /device:TPU:17, one launch (start us, length us, event | category | flops | bytes accessed | tf_op | source)
XLA Modules:
  0.0 80.5 jit_solution(746290577605197269)
XLA Ops:
  0.6 76.5 %shard_map.103 = (bf16[128,2048]{1,0:T(8,128)(2,1)}, bf16[128,2048]{1,0:T(8,128)(2,1)}, f32[48,128]{1,0:T(8,128)}) custom-call(bf16[128,2048]{1,0:T(8,128)(2,1)} %bitcast.13, s32[1,128]{1,0:T(1,128)} %bitcast.17, bf16[128,2048]{1,0:T(8,128)(2,1)} %bitcast.14, s32[1,128]{1,0:T(1,128)} %bitcast.18, bf16[128,2048]{1,0:T(8,128)(2,1)} %bitcast.15, ...), custom_call_target="tpu_custom_call" | custom-call | flops 3019898880 | bytes 2621440 | tf_op jit(solution)/shard_map/pallas_call | solution.py:471
  77.1 0.0 copy-start
  77.1 1.9 %copy.16 = bf16[1,1,128,2048]{3,2,1,0:T(8,128)(2,1)} copy(bf16[1,1,128,2048]{3,2,1,0:T(8,128)(2,1)} %bitcast.11) | data formatting | bytes 1048576
  79.1 0.0 copy-done
  79.1 0.0 copy-start.1
  79.1 0.8 copy.17
  79.9 0.0 copy-done.1
  79.9 0.6 copy.18
Async XLA Ops:
  77.1 2.0 %copy-start = (bf16[128,2048]{1,0:T(8,128)(2,1)S(1)}, bf16[128,2048]{1,0:T(8,128)(2,1)}, u32[]{:S(2)}) copy-start(bf16[128,2048]{1,0:T(8,128)(2,1)} %get-tuple-element.7) | copy-start | bytes 1572868
  79.1 0.8 copy-start.1
where the time goes:
time: 80.8 us; the launch traced here: 80.5 us
  Pallas kernels  76.5 us (95%)
  local copies, waits for them, and re-layouts  3.35 us (4%)
    pallas_call x1, Pallas kernels, local(): pl.pallas_call(functools.partial(kernel, sizes), out_shape=(jax.ShapeDtyp...  76.5 us
    unnamed x7, local copies, waits for them, and re-layouts  3.35 us

commit v1 on v0

v1 whole, which is shorter than its diff:
```python
import functools

import jax
import jax.numpy as jnp
from jax import lax
from jax.experimental import pallas as pl
from jax.experimental.pallas import tpu as pltpu
from jax.sharding import PartitionSpec as P

HEADS = 16
HEAD_DIM = 128
FEATURES = 2048
WINDOW = 512
TOK = 128
PAIR = 2 * TOK
SPAN = WINDOW + PAIR
SLOTS = HEADS // 2
AHEAD = 2
EPSILON = 1e-06
SCALE = HEAD_DIM**-0.5
MESH = pl.DeviceIdType.MESH
F32 = jnp.float32
BF16 = jnp.bfloat16
FAR, NEAR, OWN = 0, PAIR, 2 * PAIR


def sum_stages(sizes):
    stages = []
    for axis, left, stride in (("dp", sizes["dp"], 1), ("ctx", sizes["ctx"] // 2, 2)):
        while left > 1:
            factor = next(f for f in range(2, left + 1) if left % f == 0)
            stages.append((axis, stride, factor))
            left //= factor
            stride *= factor
    return stages


def dot(left, right, left_dim, right_dim):
    return lax.dot_general(
        left, right, (((left_dim,), (right_dim,)), ((), ())), preferred_element_type=F32
    )


def kernel(
    sizes,
    sec_ref,
    sec_pos,
    sav_ref,
    sav_pos,
    cot_ref,
    norm_ref,
    outg_ref,
    plan_ref,
    next_ref,
    up_ref,
    total_ref,
    keys,
    cot,
    pos,
    norm_in,
    outg_in,
    plan_in,
    gains,
    masks,
    grads,
    own,
    from_near,
    from_far,
    produced,
    dx,
    sums,
    halves,
    load_sem,
    small_sem,
    pos_sem,
    swap_recv,
    cot_recv,
    pair_recv,
    relay_recv,
    near_recv,
    far_recv,
    out_recv,
    send_sem,
    sum_send,
    sum_recv,
):
    n = sizes["ctx"]
    c = lax.axis_index("ctx")
    side = lax.rem(c, 2)
    partner = c + 1 - 2 * side
    pipe = lax.axis_index("pipe")
    after = lax.rem(pipe + 1, sizes["pipe"])
    before = lax.rem(pipe + sizes["pipe"] - 1, sizes["pipe"])
    up, down = c + 2 < n, c >= 2
    up2, down2 = c + 4 < n, c >= 4
    stages = sum_stages(sizes)
    SWAP, COT, POS, PAIRS, RELAY, NEARG, FARG, OUT, HALF = range(9)

    def part(first, which):
        return pl.ds(pl.multiple_of(first + which * TOK, TOK), TOK)

    def lanes_of(h):
        return pl.ds(pl.multiple_of(h * HEAD_DIM, HEAD_DIM), HEAD_DIM)

    def remote(source, target, send, recv, device):
        return pltpu.make_async_remote_copy(
            src_ref=source,
            dst_ref=target,
            send_sem=send,
            recv_sem=recv,
            device_id=device,
            device_id_type=MESH,
        )

    def wait_bytes(ref, sem):
        pltpu.make_async_copy(ref, ref, sem).wait()

    def load(which, j):
        source = (sav_ref, sec_ref, cot_ref)[which]
        mine = part(0, side) if which == 2 else part(OWN, side)
        target = cot.at[j, mine] if which == 2 else keys.at[which, j, mine]
        return pltpu.make_async_copy(
            source.at[:, lanes_of(side * SLOTS + j)], target, load_sem.at[which]
        )

    def swap_copy(t, j):
        mine = part(OWN, side)
        return remote(
            (sav_ref, sec_ref)[t].at[:, lanes_of((1 - side) * SLOTS + j)],
            keys.at[t, j, mine],
            send_sem.at[SWAP],
            swap_recv.at[t * SLOTS + j],
            {"ctx": partner},
        )

    def cot_copy(j):
        return remote(
            cot_ref.at[:, lanes_of((1 - side) * SLOTS + j)],
            cot.at[j, part(0, side)],
            send_sem.at[COT],
            cot_recv.at[j],
            {"ctx": partner},
        )

    def pos_copy(t):
        return remote(
            (sav_pos, sec_pos)[t],
            pos.at[t, side],
            send_sem.at[POS],
            pos_sem.at[1],
            {"ctx": partner},
        )

    def pair_copy(s, which):
        t, j = s // SLOTS, lax.rem(s, SLOTS)
        return remote(
            keys.at[t, j, part(OWN, which)],
            keys.at[t, j, part(NEAR, which)],
            send_sem.at[PAIRS],
            pair_recv.at[s],
            {"ctx": c + 2},
        )

    def relay_copy(s):
        t, j = s // SLOTS, lax.rem(s, SLOTS)
        return remote(
            keys.at[t, j, pl.ds(NEAR, PAIR)],
            keys.at[t, j, pl.ds(FAR, PAIR)],
            send_sem.at[RELAY],
            relay_recv.at[s],
            {"ctx": c + 2},
        )

    def near_copy(j):
        return remote(
            grads.at[j, pl.ds(NEAR, PAIR)],
            from_near.at[j],
            send_sem.at[NEARG],
            near_recv.at[j],
            {"ctx": c - 2},
        )

    def far_copy(j):
        return remote(
            grads.at[j, pl.ds(FAR, PAIR)],
            from_far.at[j],
            send_sem.at[FARG],
            far_recv.at[j],
            {"ctx": c - 4},
        )

    def out_copy(kind, j, which):
        device = {"pipe": (after, before)[kind]}
        if which == 1:
            device["ctx"] = partner
        rows = part(0, side if which == 0 else 1 - side)
        return remote(
            (produced, dx)[kind].at[j, rows],
            (next_ref, up_ref)[kind].at[:, lanes_of(side * SLOTS + j)],
            send_sem.at[OUT + kind],
            out_recv.at[kind],
            device,
        )

    def digit_of(stage):
        axis, stride, factor = stages[stage]
        return lax.rem(lax.axis_index(axis) // stride, factor)

    def sum_peer(stage, offset):
        axis, stride, factor = stages[stage]
        digit = digit_of(stage)
        return {axis: lax.axis_index(axis) + (lax.rem(digit + offset, factor) - digit) * stride}

    def sum_copy(stage, offset, sender):
        return remote(
            sums.at[stage, digit_of(stage)],
            sums.at[stage, sender],
            sum_send.at[stage, offset - 1],
            sum_recv.at[stage, offset - 1],
            sum_peer(stage, offset),
        )

    def half_copy():
        return remote(
            halves.at[side],
            halves.at[side],
            pos_sem.at[2],
            pos_sem.at[3],
            {"ctx": partner},
        )

    def start_sum(stage):
        for offset in range(1, stages[stage][2]):
            sum_copy(stage, offset, digit_of(stage)).start()

    def finish_sum(stage):
        factor = stages[stage][2]
        for offset in range(1, factor):
            sender = lax.rem(digit_of(stage) + factor - offset, factor)
            sum_copy(stage, offset, sender).wait_recv()
        total = sums[stage, 0]
        for digit in range(1, factor):
            total = total + sums[stage, digit]
        if stage + 1 < len(stages):
            sums[stage + 1, digit_of(stage + 1)] = total
            start_sum(stage + 1)
        else:
            finish_half(total)

    def finish_half(total):
        halves[side] = total * (1.0 / TOK)
        half_copy().start()

    def finish_total():
        half_copy().wait_recv()
        for which in range(2):
            for m in range(3):
                total_ref[pl.ds(m * HEADS + which * SLOTS, SLOTS), :] = halves[
                    which, pl.ds(m * SLOTS, SLOTS), :
                ]

    def step_sum(step):
        if step < len(stages):
            finish_sum(step)
        elif step == len(stages):
            finish_total()

    def each(action):
        @pl.loop(0, SLOTS)
        def _(j):
            action(j)

    barrier = pltpu.get_barrier_semaphore()

    def greet(device):
        pl.semaphore_signal(barrier, inc=1, device_id=device, device_id_type=MESH)

    greet({"ctx": partner})
    greet({"pipe": after})
    greet({"ctx": partner, "pipe": after})
    count = 3
    if sizes["pipe"] > 2:
        greet({"pipe": before})
        greet({"ctx": partner, "pipe": before})
        count += 2
    for condition, device in ((up, c + 2), (down, c - 2), (up2, c + 4), (down2, c - 4)):
        pl.when(condition)(lambda: greet({"ctx": device}))
        count = count + condition.astype(jnp.int32)
    for stage, (axis, stride, factor) in enumerate(stages):
        if axis == "ctx" and factor == 2 and stride <= 4:
            continue
        for offset in range(1, factor):
            greet(sum_peer(stage, offset))
            count += 1

    each(lambda j: load(0, j).start())
    small = (
        (norm_ref, norm_in),
        (outg_ref, outg_in),
        (plan_ref, plan_in),
        (sav_pos, pos.at[0, side]),
        (sec_pos, pos.at[1, side]),
    )
    for i, (source, target) in enumerate(small):
        pltpu.make_async_copy(source, target, small_sem.at[i]).start()
    each(lambda j: load(2, j).start())
    each(lambda j: load(1, j).start())
    wait_bytes(keys.at[0, :, pl.ds(0, TOK)], load_sem.at[0])
    pl.semaphore_wait(barrier, count)

    def pass_pair(s, which):
        pl.when(up)(lambda: pair_copy(s, which).start())

    def relay(s):
        @pl.when(down)
        def _():
            wait_bytes(keys.at[0, 0, pl.ds(NEAR, PAIR)], pair_recv.at[s])
            pl.when(up)(lambda: relay_copy(s).start())

    def wait_swap(s):
        wait_bytes(keys.at[0, 0, pl.ds(0, TOK)], swap_recv.at[s])

    for t in range(2):
        pos_copy(t).start()

    def first_swaps(j):
        swap_copy(0, j).start()
        pl.when(j < AHEAD)(lambda: pass_pair(j, side))
        cot_copy(j).start()

    each(first_swaps)
    each(lambda j: swap_copy(1, j).start())

    for i, (source, target) in enumerate(small):
        pltpu.make_async_copy(source, target, small_sem.at[i]).wait()
    for which in range(2):
        lap = plan_in[0, which]
        gains[pl.ds(3 * which, 2), :] = jnp.where(lap == 1, norm_in[1], norm_in[0])
        gains[pl.ds(3 * which + 2, 1), :] = jnp.where(lap == 1, outg_in[1], outg_in[0])
    for reach, first in ((2, NEAR), (4, FAR)):

        @pl.when(c < reach)
        def _():
            @pl.loop(0, SLOTS)
            def _(j):
                for t in range(2):
                    keys[t, j, pl.ds(first, PAIR)] = jnp.zeros((PAIR, HEAD_DIM), BF16)

    for s in range(AHEAD):
        wait_swap(s)
        pass_pair(s, 1 - side)

    wait_bytes(pos.at[:, 0], pos_sem.at[1])
    distance = (
        lax.broadcasted_iota(jnp.int32, (SPAN, TOK), 1)
        + WINDOW
        - lax.broadcasted_iota(jnp.int32, (SPAN, TOK), 0)
    )
    for t in range(2):
        for which in range(2):
            apart = distance + which * TOK
            allowed = (apart >= 0) & (apart < WINDOW) & (apart <= pos[t, which])
            masks[t, :, pl.ds(which * TOK, TOK)] = jnp.where(allowed, 1.0, 0.0).astype(F32)

    wait_bytes(cot.at[:, pl.ds(0, TOK)], load_sem.at[2])
    wait_bytes(keys.at[1, :, pl.ds(0, TOK)], load_sem.at[1])
    relay(0)

    def normed(x):
        wide = x.astype(F32)
        inverse = lax.rsqrt(jnp.mean(wide * wide, axis=-1, keepdims=True) + EPSILON)
        return wide * inverse, inverse

    def weights(t, n_all, a, b):
        k = (n_all * b).astype(BF16)
        q = (n_all[WINDOW:] * a).astype(BF16)
        w = jnp.exp(dot(k, q, 1, 1) * SCALE) * masks[t]
        prob = w * (1.0 / jnp.sum(w, axis=0, keepdims=True))
        return q, k, prob

    sum_slot = digit_of(0) if stages else 0

    def backward(j):
        wide = lanes_of(side * SLOTS + j)
        a, b, g = (gains[pl.ds(3 + m, 1), wide] for m in range(3))
        x = keys[0, j]
        n_all, inverse = normed(x)
        q, k, prob = weights(0, n_all, a, b)
        p = prob.astype(BF16)
        ct = cot[j].astype(F32)
        d_mix = (ct * g).astype(BF16)
        d_prob = dot(x, d_mix, 1, 1)
        delta = jnp.sum(prob * d_prob, axis=0, keepdims=True)
        d_score = (prob * (d_prob - delta)).astype(BF16)
        mix = dot(p, x, 0, 0)
        d_k = dot(d_score, q, 1, 0)
        d_q = dot(d_score, k, 0, 0)
        d_value = dot(p, d_mix, 1, 0)
        n_own = n_all[WINDOW:]
        d_n = d_k * (b * SCALE)
        d_n_own = d_n[WINDOW:] + d_q * (a * SCALE)

        def through_norm(d, value, scale):
            return scale * (d - value * jnp.mean(d * value, axis=-1, keepdims=True))

        grads[j] = (
            d_value[:WINDOW] + through_norm(d_n[:WINDOW], n_all[:WINDOW], inverse[:WINDOW])
        ).astype(BF16)
        own[j] = d_value[WINDOW:] + through_norm(d_n_own, n_own, inverse[WINDOW:]) + ct
        parts = (
            jnp.sum(d_q * n_own, axis=0, keepdims=True) * SCALE,
            jnp.sum(d_k * n_all, axis=0, keepdims=True) * SCALE,
            jnp.sum(ct * mix, axis=0, keepdims=True),
        )
        for m in range(3):
            sums[0, sum_slot, pl.ds(m * SLOTS + j, 1), :] = parts[m]

    def forward(j):
        wide = lanes_of(side * SLOTS + j)
        a, b, g = (gains[pl.ds(m, 1), wide] for m in range(3))
        x = keys[1, j]
        n_all, _ = normed(x)
        _, _, prob = weights(1, n_all, a, b)
        mix = dot(prob.astype(BF16), x, 0, 0)
        produced[j] = (x[WINDOW:].astype(F32) + g * mix).astype(BF16)

    def feed(s, total):
        @pl.when(s + AHEAD < total)
        def _():
            wait_swap(s + AHEAD)
            pass_pair(s + AHEAD, side)
            pass_pair(s + AHEAD, 1 - side)

        pl.when(s + 1 < total)(lambda: relay(s + 1))
        pl.when(down2)(lambda: wait_bytes(keys.at[0, 0, pl.ds(FAR, PAIR)], relay_recv.at[s]))

    def first(j):
        feed(j, 2 * SLOTS)
        wait_bytes(cot.at[0, pl.ds(0, TOK)], cot_recv.at[j])
        backward(j)
        pl.when(down)(lambda: near_copy(j).start())
        pl.when(down2)(lambda: far_copy(j).start())

    each(first)
    if stages:
        start_sum(0)
    else:
        finish_half(sums[0, 0])

    def send_dx(j):
        @pl.when(up)
        def _():
            near_copy(j).wait_recv()
            own[j] = own[j] + from_near[j].astype(F32)

        @pl.when(up2)
        def _():
            far_copy(j).wait_recv()
            own[j] = own[j] + from_far[j].astype(F32)

        dx[j] = own[j].astype(BF16)
        for which in range(2):
            out_copy(1, j, which).start()

    def last(j):
        feed(j + SLOTS, 2 * SLOTS)
        forward(j)
        for which in range(2):
            out_copy(0, j, which).start()
        for step in range(min(SLOTS, len(stages) + 1)):
            pl.when(j == step)(lambda: step_sum(step))
        send_dx(j)

    each(last)
    for step in range(SLOTS, len(stages) + 1):
        step_sum(step)

    swapped = keys.at[:, :, pl.ds(0, TOK)]
    paired = keys.at[:, :, pl.ds(0, PAIR)]
    wait_bytes(swapped, send_sem.at[SWAP])
    wait_bytes(cot.at[:, pl.ds(0, TOK)], send_sem.at[COT])
    wait_bytes(pos.at[:, 0], send_sem.at[POS])
    pl.when(up)(lambda: wait_bytes(paired, send_sem.at[PAIRS]))
    pl.when(up & down)(lambda: wait_bytes(paired, send_sem.at[RELAY]))
    pl.when(down)(lambda: wait_bytes(from_near, send_sem.at[NEARG]))
    pl.when(down2)(lambda: wait_bytes(from_far, send_sem.at[FARG]))
    half_copy().wait_send()
    for stage, (_, _, factor) in enumerate(stages):
        for offset in range(1, factor):
            sum_copy(stage, offset, digit_of(stage)).wait_send()
    for kind, (sent, target) in enumerate(((produced, next_ref), (dx, up_ref))):
        wait_bytes(sent, send_sem.at[OUT + kind])
        wait_bytes(target, out_recv.at[kind])


def local(
    sizes,
    section_input,
    section_positions,
    saved_input,
    saved_positions,
    cotangent,
    norm_gains,
    output_gains,
    plan,
):
    stages = sum_stages(sizes)
    widest = max([factor for _, _, factor in stages] + [2])
    depth = max(len(stages), 1)
    anywhere = pl.BlockSpec(memory_space=pl.ANY)
    in_vmem = pl.BlockSpec(memory_space=pltpu.VMEM)
    produced, grads, totals = pl.pallas_call(
        functools.partial(kernel, sizes),
        out_shape=(
            jax.ShapeDtypeStruct((TOK, FEATURES), BF16),
            jax.ShapeDtypeStruct((TOK, FEATURES), BF16),
            jax.ShapeDtypeStruct((3 * HEADS, HEAD_DIM), F32),
        ),
        in_specs=[anywhere] * 8,
        out_specs=(anywhere, anywhere, in_vmem),
        scratch_shapes=[
            pltpu.VMEM((2, SLOTS, SPAN, HEAD_DIM), BF16),
            pltpu.VMEM((SLOTS, PAIR, HEAD_DIM), BF16),
            pltpu.VMEM((2, 2, 1, TOK), jnp.int32),
            pltpu.VMEM((2, 2, FEATURES), F32),
            pltpu.VMEM((2, 1, FEATURES), F32),
            pltpu.SMEM((1, 2), jnp.int32),
            pltpu.VMEM((8, FEATURES), F32),
            pltpu.VMEM((2, SPAN, PAIR), F32),
            pltpu.VMEM((SLOTS, WINDOW, HEAD_DIM), BF16),
            pltpu.VMEM((SLOTS, PAIR, HEAD_DIM), F32),
            pltpu.VMEM((SLOTS, PAIR, HEAD_DIM), BF16),
            pltpu.VMEM((SLOTS, PAIR, HEAD_DIM), BF16),
            pltpu.VMEM((SLOTS, PAIR, HEAD_DIM), BF16),
            pltpu.VMEM((SLOTS, PAIR, HEAD_DIM), BF16),
            pltpu.VMEM((depth, widest, 3 * SLOTS, HEAD_DIM), F32),
            pltpu.VMEM((2, 3 * SLOTS, HEAD_DIM), F32),
            pltpu.SemaphoreType.DMA((3,)),
            pltpu.SemaphoreType.DMA((5,)),
            pltpu.SemaphoreType.DMA((4,)),
            pltpu.SemaphoreType.DMA((2 * SLOTS,)),
            pltpu.SemaphoreType.DMA((SLOTS,)),
            pltpu.SemaphoreType.DMA((2 * SLOTS,)),
            pltpu.SemaphoreType.DMA((2 * SLOTS,)),
            pltpu.SemaphoreType.DMA((SLOTS,)),
            pltpu.SemaphoreType.DMA((SLOTS,)),
            pltpu.SemaphoreType.DMA((2,)),
            pltpu.SemaphoreType.DMA((9,)),
            pltpu.SemaphoreType.DMA((depth, widest - 1)),
            pltpu.SemaphoreType.DMA((depth, widest - 1)),
        ],
        compiler_params=pltpu.CompilerParams(
            collective_id=0, has_side_effects=True, vmem_limit_bytes=24 * 1024 * 1024
        ),
        cost_estimate=pl.CostEstimate(
            flops=9 * 2 * TOK * SPAN * FEATURES,
            bytes_accessed=5 * TOK * FEATURES * 2,
            transcendentals=2 * HEADS * TOK * SPAN,
        ),
    )(
        section_input[0, 0],
        section_positions[0],
        saved_input[0, 0],
        saved_positions[0],
        cotangent[0, 0],
        norm_gains[:, 0],
        output_gains,
        plan[0],
    )
    return (produced[None, None], grads[None, None], totals.reshape(1, 3, FEATURES))


def solution(mesh):
    placed = (
        P("dp", "pipe", "ctx", None),
        P("dp", "pipe", "ctx"),
        P("dp", "pipe", "ctx", None),
        P("dp", "pipe", "ctx"),
        P("dp", "pipe", "ctx", None),
        P(None, "pipe", None, None),
        P(None, "pipe", None),
        P("dp", "pipe", None),
    )
    return jax.shard_map(
        functools.partial(local, {axis: mesh.shape[axis] for axis in ("dp", "pipe", "ctx")}),
        mesh=mesh,
        in_specs=placed,
        out_specs=(
            P("dp", "pipe", "ctx", None),
            P("dp", "pipe", "ctx", None),
            P("pipe", None, None),
        ),
        check_vma=False,
    )
```

time: 80.8 us -> 71 us (0.88)
  Pallas kernels: 76.5 us -> 62.3 us
  local copies, waits for them, and re-layouts: 3.35 us -> 7.46 us
    pallas_call x1, Pallas kernels: 76.5 us -> 62.3 us  [local(): pl.pallas_call(functools.partial(kernel, sizes), out_shape=(jax.ShapeDtyp...]
    unnamed x7 -> x19, local copies, waits for them, and re-layouts: 3.35 us -> 7.46 us
where the time goes in v1:
time: 71 us; the launch traced here: 70.4 us
  Pallas kernels  62.3 us (88%)
  local copies, waits for them, and re-layouts  7.46 us (11%)
    pallas_call x1, Pallas kernels, local(): pl.pallas_call(functools.partial(kernel, sizes), out_shape=(jax.ShapeDtyp...  62.3 us
    unnamed x19, local copies, waits for them, and re-layouts  7.46 us

profile of v1, /device:TPU:17, one launch (start us, length us, event | category | flops | bytes accessed | tf_op | source)
XLA Modules:
  0.0 70.4 jit_solution(11214031233284890277)
XLA Ops:
  0.6 0.0 copy-start.5
  0.6 0.0 copy-start.6
  0.7 0.0 copy-start.7
  0.7 0.6 copy-done.5
  1.3 0.0 copy-done.6
  1.3 0.0 copy-done.7
  1.3 0.0 copy-start
  1.3 1.0 %copy-done = bf16[1,1,128,2048]{3,2,1,0:T(8,128)(2,1)S(1)} copy-done((bf16[1,1,128,2048]{3,2,1,0:T(8,128)(2,1)S(1)}, bf16[1,1,128,2048]{3,2,1,0:T(8,128)(2,1)}, u32[]{:S(2)}) %copy-start) | copy-done | bytes 524312
  2.4 0.0 copy-start.1
  2.4 1.0 %copy-done.1 = bf16[1,1,128,2048]{3,2,1,0:T(8,128)(2,1)S(1)} copy-done((bf16[1,1,128,2048]{3,2,1,0:T(8,128)(2,1)S(1)}, bf16[1,1,128,2048]{3,2,1,0:T(8,128)(2,1)}, u32[]{:S(2)}) %copy-start.1) | copy-done | bytes 524312
  3.4 0.0 copy-start.2
  3.4 1.0 %copy-done.2 = bf16[1,1,128,2048]{3,2,1,0:T(8,128)(2,1)S(1)} copy-done((bf16[1,1,128,2048]{3,2,1,0:T(8,128)(2,1)S(1)}, bf16[1,1,128,2048]{3,2,1,0:T(8,128)(2,1)}, u32[]{:S(2)}) %copy-start.2) | copy-done | bytes 524312
  4.4 0.0 copy-start.3
  4.4 0.8 %copy-done.3 = f32[2,1,2,2048]{3,2,1,0:T(2,128)S(1)} copy-done((f32[2,1,2,2048]{3,2,1,0:T(2,128)S(1)}, f32[2,1,2,2048]{3,2,1,0:T(2,128)}, u32[]{:S(2)}) %copy-start.3) | copy-done | bytes 32792
  5.2 0.0 copy-start.4
  5.2 0.7 %copy-done.4 = f32[2,1,2048]{2,1,0:T(1,128)S(1)} copy-done((f32[2,1,2048]{2,1,0:T(1,128)S(1)}, f32[2,1,2048]{2,1,0:T(1,128)}, u32[]{:S(2)}) %copy-start.4) | copy-done | bytes 16408
  5.9 62.3 %shard_map.103 = (bf16[128,2048]{1,0:T(8,128)(2,1)S(1)}, bf16[128,2048]{1,0:T(8,128)(2,1)S(1)}, f32[48,128]{1,0:T(8,128)S(1)}) custom-call(bf16[128,2048]{1,0:T(8,128)(2,1)S(1)} %bitcast.13, s32[1,128]{1,0:T(1,128)S(1)} %bitcast.17, bf16[128,2048]{1,0:T(8,128)(2,1)S(1)} %bitcast.14, s32[1,128]{1,0:T(1,128)S(1)} %bitcast.18, bf16[128,2048]{1,0:T(8,128)(2,1)S(1)} %bitcast.15, ...), custom_call_target="tpu_custom_call" | custom-call | flops 3623878656 | bytes 2621440 | tf_op jit(solution)/shard_map/pallas_call | solution.py:512
  68.2 0.8 %copy.16 = bf16[1,1,128,2048]{3,2,1,0:T(8,128)(2,1)} copy(bf16[1,1,128,2048]{3,2,1,0:T(8,128)(2,1)S(1)} %bitcast.11) | data formatting | bytes 1048576
  69.0 0.8 %copy.17 = bf16[1,1,128,2048]{3,2,1,0:T(8,128)(2,1)} copy(bf16[1,1,128,2048]{3,2,1,0:T(8,128)(2,1)S(1)} %bitcast.10) | data formatting | bytes 1048576
  69.8 0.6 copy.18
Async XLA Ops:
  0.6 0.7 copy-start.5
  0.6 0.7 copy-start.6
  0.7 0.7 copy-start.7
  1.3 1.0 %copy-start = (bf16[1,1,128,2048]{3,2,1,0:T(8,128)(2,1)S(1)}, bf16[1,1,128,2048]{3,2,1,0:T(8,128)(2,1)}, u32[]{:S(2)}) copy-start(bf16[1,1,128,2048]{3,2,1,0:T(8,128)(2,1)} %param.8) | copy-start | bytes 1572868
  2.4 1.0 %copy-start.1 = (bf16[1,1,128,2048]{3,2,1,0:T(8,128)(2,1)S(1)}, bf16[1,1,128,2048]{3,2,1,0:T(8,128)(2,1)}, u32[]{:S(2)}) copy-start(bf16[1,1,128,2048]{3,2,1,0:T(8,128)(2,1)} %param.10) | copy-start | bytes 1572868
  3.4 1.0 %copy-start.2 = (bf16[1,1,128,2048]{3,2,1,0:T(8,128)(2,1)S(1)}, bf16[1,1,128,2048]{3,2,1,0:T(8,128)(2,1)}, u32[]{:S(2)}) copy-start(bf16[1,1,128,2048]{3,2,1,0:T(8,128)(2,1)} %param.12) | copy-start | bytes 1572868
  4.4 0.8 %copy-start.3 = (f32[2,1,2,2048]{3,2,1,0:T(2,128)S(1)}, f32[2,1,2,2048]{3,2,1,0:T(2,128)}, u32[]{:S(2)}) copy-start(f32[2,1,2,2048]{3,2,1,0:T(2,128)} %param.13) | copy-start | bytes 98308
  5.2 0.7 %copy-start.4 = (f32[2,1,2048]{2,1,0:T(1,128)S(1)}, f32[2,1,2048]{2,1,0:T(1,128)}, u32[]{:S(2)}) copy-start(f32[2,1,2048]{2,1,0:T(1,128)} %outg_ref.1) | copy-start | bytes 49156

commit v2 on v1

--- a/solution.py
+++ b/solution.py
@@ -15,9 +15,13 @@
 PAIR = 2 * TOK
 SPAN = WINDOW + PAIR
 SLOTS = HEADS // 2
-AHEAD = 2
+OWN_AHEAD = 5
+AHEAD = 3
+PASS = 2
+DELAY = 4
 EPSILON = 1e-06
 SCALE = HEAD_DIM**-0.5
+LOG2E = 1.4426950408889634
 MESH = pl.DeviceIdType.MESH
 F32 = jnp.float32
 BF16 = jnp.bfloat16
@@ -26,12 +30,12 @@
 
 def sum_stages(sizes):
     stages = []
-    for axis, left, stride in (("dp", sizes["dp"], 1), ("ctx", sizes["ctx"] // 2, 2)):
-        while left > 1:
-            factor = next(f for f in range(2, left + 1) if left % f == 0)
-            stages.append((axis, stride, factor))
-            left //= factor
-            stride *= factor
+    left, stride = sizes["dp"], 1
+    while left > 1:
+        factor = next(f for f in range(2, left + 1) if left % f == 0)
+        stages.append(("dp", stride, factor))
+        left //= factor
+        stride *= factor
     return stages
 
 
@@ -69,6 +73,7 @@
     produced,
     dx,
     sums,
+    columns,
     halves,
     load_sem,
     small_sem,
@@ -83,6 +88,7 @@
     send_sem,
     sum_send,
     sum_recv,
+    column_recv,
 ):
     n = sizes["ctx"]
     c = lax.axis_index("ctx")
@@ -92,9 +98,10 @@
     after = lax.rem(pipe + 1, sizes["pipe"])
     before = lax.rem(pipe + sizes["pipe"] - 1, sizes["pipe"])
     up, down = c + 2 < n, c >= 2
-    up2, down2 = c + 4 < n, c >= 4
+    down2 = c >= 4
+    level, levels = c // 2, n // 2
     stages = sum_stages(sizes)
-    SWAP, COT, POS, PAIRS, RELAY, NEARG, FARG, OUT, HALF = range(9)
+    SWAP, COT, POS, PAIRS, RELAY, NEARG, FARG, OUT = range(8)
 
     def part(first, which):
         return pl.ds(pl.multiple_of(first + which * TOK, TOK), TOK)
@@ -186,7 +193,7 @@
             from_far.at[j],
             send_sem.at[FARG],
             far_recv.at[j],
-            {"ctx": c - 4},
+            {"ctx": c - 2},
         )
 
     def out_copy(kind, j, which):
@@ -245,7 +252,40 @@
             sums[stage + 1, digit_of(stage + 1)] = total
             start_sum(stage + 1)
         else:
-            finish_half(total)
+            start_column(total)
+
+    def column_copy(which, step):
+        return remote(
+            columns.at[which],
+            columns.at[which],
+            pos_sem.at[4],
+            column_recv.at[which],
+            {"ctx": c + step},
+        )
+
+    def start_column(total):
+        columns[level] = total
+        pl.when(up)(lambda: column_copy(level, 2).start())
+        pl.when(down)(lambda: column_copy(level, -2).start())
+
+    def pass_column(k):
+        below, above = level - k, level + k
+
+        @pl.when(below >= 0)
+        def _():
+            wait_bytes(columns.at[0], column_recv.at[below])
+            pl.when(up)(lambda: column_copy(below, 2).start())
+
+        @pl.when(above < levels)
+        def _():
+            wait_bytes(columns.at[0], column_recv.at[above])
+            pl.when(down)(lambda: column_copy(above, -2).start())
+
+    def finish_column():
+        total = columns[0]
+        for which in range(1, levels):
+            total = total + columns[which]
+        finish_half(total)
 
     def finish_half(total):
         halves[side] = total * (1.0 / TOK)
@@ -259,11 +299,15 @@
                     which, pl.ds(m * SLOTS, SLOTS), :
                 ]
 
-    def step_sum(step):
-        if step < len(stages):
-            finish_sum(step)
-        elif step == len(stages):
-            finish_total()
+    steps = [functools.partial(finish_sum, stage) for stage in range(len(stages))]
+    steps += [functools.partial(pass_column, k) for k in range(1, levels)]
+
+    def last_column():
+        pass_column(levels - 1)
+        finish_column()
+
+    steps[-1] = last_column
+    steps.append(finish_total)
 
     def each(action):
         @pl.loop(0, SLOTS)
@@ -283,12 +327,10 @@
         greet({"pipe": before})
         greet({"ctx": partner, "pipe": before})
         count += 2
-    for condition, device in ((up, c + 2), (down, c - 2), (up2, c + 4), (down2, c - 4)):
+    for condition, device in ((up, c + 2), (down, c - 2)):
         pl.when(condition)(lambda: greet({"ctx": device}))
         count = count + condition.astype(jnp.int32)
-    for stage, (axis, stride, factor) in enumerate(stages):
-        if axis == "ctx" and factor == 2 and stride <= 4:
-            continue
+    for stage, (_, _, factor) in enumerate(stages):
         for offset in range(1, factor):
             greet(sum_peer(stage, offset))
             count += 1
@@ -325,7 +367,7 @@
 
     def first_swaps(j):
         swap_copy(0, j).start()
-        pl.when(j < AHEAD)(lambda: pass_pair(j, side))
+        pl.when(j < OWN_AHEAD)(lambda: pass_pair(j, side))
         cot_copy(j).start()
 
     each(first_swaps)
@@ -364,19 +406,17 @@
 
     wait_bytes(cot.at[:, pl.ds(0, TOK)], load_sem.at[2])
     wait_bytes(keys.at[1, :, pl.ds(0, TOK)], load_sem.at[1])
-    relay(0)
+    for s in range(PASS):
+        relay(s)
 
     def normed(x):
         wide = x.astype(F32)
         inverse = lax.rsqrt(jnp.mean(wide * wide, axis=-1, keepdims=True) + EPSILON)
         return wide * inverse, inverse
 
-    def weights(t, n_all, a, b):
-        k = (n_all * b).astype(BF16)
-        q = (n_all[WINDOW:] * a).astype(BF16)
-        w = jnp.exp(dot(k, q, 1, 1) * SCALE) * masks[t]
-        prob = w * (1.0 / jnp.sum(w, axis=0, keepdims=True))
-        return q, k, prob
+    def probability(t, k, q, queries):
+        w = jnp.exp2(dot(k, q, 1, 1) * (SCALE * LOG2E)) * masks[t, :, queries]
+        return w * (1.0 / jnp.sum(w, axis=0, keepdims=True))
 
     sum_slot = digit_of(0) if stages else 0
 
@@ -385,17 +425,19 @@
         a, b, g = (gains[pl.ds(3 + m, 1), wide] for m in range(3))
         x = keys[0, j]
         n_all, inverse = normed(x)
-        q, k, prob = weights(0, n_all, a, b)
+        k = (n_all * b).astype(BF16)
+        q = (n_all[WINDOW:] * a).astype(BF16)
+        prob = probability(0, k, q, pl.ds(0, PAIR))
         p = prob.astype(BF16)
         ct = cot[j].astype(F32)
         d_mix = (ct * g).astype(BF16)
         d_prob = dot(x, d_mix, 1, 1)
         delta = jnp.sum(prob * d_prob, axis=0, keepdims=True)
         d_score = (prob * (d_prob - delta)).astype(BF16)
-        mix = dot(p, x, 0, 0)
         d_k = dot(d_score, q, 1, 0)
-        d_q = dot(d_score, k, 0, 0)
-        d_value = dot(p, d_mix, 1, 0)
+        d_q = dot(k, d_score, 0, 0).T
+        mixed = dot(p, cot[j], 1, 0)
+        d_value = mixed * g
         n_own = n_all[WINDOW:]
         d_n = d_k * (b * SCALE)
         d_n_own = d_n[WINDOW:] + d_q * (a * SCALE)
@@ -410,7 +452,7 @@
         parts = (
             jnp.sum(d_q * n_own, axis=0, keepdims=True) * SCALE,
             jnp.sum(d_k * n_all, axis=0, keepdims=True) * SCALE,
-            jnp.sum(ct * mix, axis=0, keepdims=True),
+            jnp.sum(mixed * x, axis=0, keepdims=True),
         )
         for m in range(3):
             sums[0, sum_slot, pl.ds(m * SLOTS + j, 1), :] = parts[m]
@@ -419,33 +461,48 @@
         wide = lanes_of(side * SLOTS + j)
         a, b, g = (gains[pl.ds(m, 1), wide] for m in range(3))
         x = keys[1, j]
-        n_all, _ = normed(x)
-        _, _, prob = weights(1, n_all, a, b)
-        mix = dot(prob.astype(BF16), x, 0, 0)
-        produced[j] = (x[WINDOW:].astype(F32) + g * mix).astype(BF16)
+        k = (normed(x)[0] * b).astype(BF16)
+        for which in (1, 0):
+            rows = side if which == 0 else 1 - side
+            mine = keys[1, j, part(OWN, rows)]
+            q = (normed(mine)[0] * a).astype(BF16)
+            prob = probability(1, k, q, part(0, rows))
+            mix = dot(x, prob.astype(BF16), 0, 0).T
+            produced[j, part(0, rows)] = (mine.astype(F32) + g * mix).astype(BF16)
+            out_copy(0, j, which).start()
 
     def feed(s, total):
         @pl.when(s + AHEAD < total)
         def _():
             wait_swap(s + AHEAD)
-            pass_pair(s + AHEAD, side)
             pass_pair(s + AHEAD, 1 - side)
 
-        pl.when(s + 1 < total)(lambda: relay(s + 1))
+        pl.when(s + OWN_AHEAD < total)(lambda: pass_pair(s + OWN_AHEAD, side))
+
+        pl.when(s + PASS < total)(lambda: relay(s + PASS))
         pl.when(down2)(lambda: wait_bytes(keys.at[0, 0, pl.ds(FAR, PAIR)], relay_recv.at[s]))
+
+    def send_near(j):
+        @pl.when(up & down)
+        def _():
+            far_copy(j).wait_recv()
+            near = grads[j, pl.ds(NEAR, PAIR)].astype(F32) + from_far[j].astype(F32)
+            grads[j, pl.ds(NEAR, PAIR)] = near.astype(BF16)
+            near_copy(j).start()
 
     def first(j):
         feed(j, 2 * SLOTS)
         wait_bytes(cot.at[0, pl.ds(0, TOK)], cot_recv.at[j])
         backward(j)
-        pl.when(down)(lambda: near_copy(j).start())
         pl.when(down2)(lambda: far_copy(j).start())
+        pl.when(down & jnp.logical_not(up))(lambda: near_copy(j).start())
+        pl.when(j >= DELAY)(lambda: send_near(jnp.maximum(j - DELAY, 0)))
 
     each(first)
     if stages:
         start_sum(0)
     else:
-        finish_half(sums[0, 0])
+        start_column(sums[0, 0])
 
     def send_dx(j):
         @pl.when(up)
@@ -453,27 +510,21 @@
             near_copy(j).wait_recv()
             own[j] = own[j] + from_near[j].astype(F32)
 
-        @pl.when(up2)
-        def _():
-            far_copy(j).wait_recv()
-            own[j] = own[j] + from_far[j].astype(F32)
-
         dx[j] = own[j].astype(BF16)
         for which in range(2):
             out_copy(1, j, which).start()
 
     def last(j):
+        pl.when(j < DELAY)(lambda: send_near(jnp.minimum(j + SLOTS - DELAY, SLOTS - 1)))
+        send_dx(j)
+        for i, step in enumerate(steps[:SLOTS]):
+            pl.when(j == i)(step)
         feed(j + SLOTS, 2 * SLOTS)
         forward(j)
-        for which in range(2):
-            out_copy(0, j, which).start()
-        for step in range(min(SLOTS, len(stages) + 1)):
-            pl.when(j == step)(lambda: step_sum(step))
-        send_dx(j)
 
     each(last)
-    for step in range(SLOTS, len(stages) + 1):
-        step_sum(step)
+    for step in steps[SLOTS:]:
+        step()
 
     swapped = keys.at[:, :, pl.ds(0, TOK)]
     paired = keys.at[:, :, pl.ds(0, PAIR)]
@@ -484,6 +535,13 @@
     pl.when(up & down)(lambda: wait_bytes(paired, send_sem.at[RELAY]))
     pl.when(down)(lambda: wait_bytes(from_near, send_sem.at[NEARG]))
     pl.when(down2)(lambda: wait_bytes(from_far, send_sem.at[FARG]))
+    upward = jnp.where(up, level + 1, 0)
+    downward = jnp.where(down, levels - level, 0)
+
+    @pl.loop(0, upward + downward)
+    def _(_i):
+        wait_bytes(columns.at[0], pos_sem.at[4])
+
     half_copy().wait_send()
     for stage, (_, _, factor) in enumerate(stages):
         for offset in range(1, factor):
@@ -491,6 +549,18 @@
     for kind, (sent, target) in enumerate(((produced, next_ref), (dx, up_ref))):
         wait_bytes(sent, send_sem.at[OUT + kind])
         wait_bytes(target, out_recv.at[kind])
+
+
+def place(produced_ref, grads_ref, total_ref, next_ref, up_ref, gain_ref, sem):
+    pairs = ((produced_ref, next_ref), (grads_ref, up_ref), (total_ref, gain_ref))
+    copies = [
+        pltpu.make_async_copy(source, target, sem.at[i])
+        for i, (source, target) in enumerate(pairs)
+    ]
+    for copy in copies:
+        copy.start()
+    for copy in copies:
+        copy.wait()
 
 
 def local(
@@ -507,15 +577,17 @@
     stages = sum_stages(sizes)
     widest = max([factor for _, _, factor in stages] + [2])
     depth = max(len(stages), 1)
+    levels = sizes["ctx"] // 2
     anywhere = pl.BlockSpec(memory_space=pl.ANY)
     in_vmem = pl.BlockSpec(memory_space=pltpu.VMEM)
-    produced, grads, totals = pl.pallas_call(
+    shapes = (
+        jax.ShapeDtypeStruct((TOK, FEATURES), BF16),
+        jax.ShapeDtypeStruct((TOK, FEATURES), BF16),
+        jax.ShapeDtypeStruct((3 * HEADS, HEAD_DIM), F32),
+    )
+    results = pl.pallas_call(
         functools.partial(kernel, sizes),
-        out_shape=(
-            jax.ShapeDtypeStruct((TOK, FEATURES), BF16),
-            jax.ShapeDtypeStruct((TOK, FEATURES), BF16),
-            jax.ShapeDtypeStruct((3 * HEADS, HEAD_DIM), F32),
-        ),
+        out_shape=shapes,
         in_specs=[anywhere] * 8,
         out_specs=(anywhere, anywhere, in_vmem),
         scratch_shapes=[
@@ -534,10 +606,11 @@
             pltpu.VMEM((SLOTS, PAIR, HEAD_DIM), BF16),
             pltpu.VMEM((SLOTS, PAIR, HEAD_DIM), BF16),
             pltpu.VMEM((depth, widest, 3 * SLOTS, HEAD_DIM), F32),
+            pltpu.VMEM((levels, 3 * SLOTS, HEAD_DIM), F32),
             pltpu.VMEM((2, 3 * SLOTS, HEAD_DIM), F32),
             pltpu.SemaphoreType.DMA((3,)),
             pltpu.SemaphoreType.DMA((5,)),
-            pltpu.SemaphoreType.DMA((4,)),
+            pltpu.SemaphoreType.DMA((5,)),
             pltpu.SemaphoreType.DMA((2 * SLOTS,)),
             pltpu.SemaphoreType.DMA((SLOTS,)),
             pltpu.SemaphoreType.DMA((2 * SLOTS,)),
@@ -548,6 +621,7 @@
             pltpu.SemaphoreType.DMA((9,)),
             pltpu.SemaphoreType.DMA((depth, widest - 1)),
             pltpu.SemaphoreType.DMA((depth, widest - 1)),
+            pltpu.SemaphoreType.DMA((levels,)),
         ],
         compiler_params=pltpu.CompilerParams(
             collective_id=0, has_side_effects=True, vmem_limit_bytes=24 * 1024 * 1024
@@ -558,15 +632,28 @@
             transcendentals=2 * HEADS * TOK * SPAN,
         ),
     )(
-        section_input[0, 0],
-        section_positions[0],
-        saved_input[0, 0],
-        saved_positions[0],
-        cotangent[0, 0],
-        norm_gains[:, 0],
-        output_gains,
-        plan[0],
+        *(
+            pltpu.with_memory_space_constraint(array, pltpu.MemorySpace.HBM)
+            for array in (
+                section_input[0, 0],
+                section_positions[0],
+                saved_input[0, 0],
+                saved_positions[0],
+                cotangent[0, 0],
+                norm_gains[:, 0],
+                output_gains,
+                plan[0],
+            )
+        )
     )
+    produced, grads, totals = pl.pallas_call(
+        place,
+        out_shape=shapes,
+        in_specs=[anywhere] * 3,
+        out_specs=(anywhere,) * 3,
+        scratch_shapes=[pltpu.SemaphoreType.DMA((3,))],
+        compiler_params=pltpu.CompilerParams(vmem_limit_bytes=1024 * 1024),
+    )(*results)
     return (produced[None, None], grads[None, None], totals.reshape(1, 3, FEATURES))
 
 

time: 71 us -> 60 us (0.85)
  local copies, waits for them, and re-layouts: 7.46 us -> 0 us
  Pallas kernels: 62.3 us -> 58.9 us
    unnamed x19 -> x0, local copies, waits for them, and re-layouts: 7.46 us -> none
    pallas_call x1 -> x2, Pallas kernels: 62.3 us -> 58.9 us  [the longest x1 57.9 us: local(): pl.pallas_call(functools.partial(kernel, sizes), out_shape=shapes, in_spe...]
where the time goes in v2:
time: 60 us; the launch traced here: 59.6 us
  Pallas kernels  58.9 us (98%)
  between operations  0.64 us (1%)
    pallas_call x1, Pallas kernels, local(): pl.pallas_call(functools.partial(kernel, sizes), out_shape=shapes, in_spe...  57.9 us

profile of v2, /device:TPU:17, one launch (start us, length us, event | category | flops | bytes accessed | tf_op | source)
XLA Modules:
  0.0 59.6 jit_solution(5627914055223628445)
XLA Ops:
  0.6 57.9 %shard_map.103 = (bf16[128,2048]{1,0:T(8,128)(2,1)S(1)}, bf16[128,2048]{1,0:T(8,128)(2,1)S(1)}, f32[48,128]{1,0:T(8,128)S(1)}) custom-call(bf16[128,2048]{1,0:T(8,128)(2,1)} %bitcast.10, s32[1,128]{1,0:T(1,128)} %bitcast.17, bf16[128,2048]{1,0:T(8,128)(2,1)} %bitcast.11, s32[1,128]{1,0:T(1,128)} %bitcast.18, bf16[128,2048]{1,0:T(8,128)(2,1)} %bitcast.12, ...), custom_call_target="tpu_custom_call" | custom-call | flops 3623878656 | bytes 2621440 | tf_op jit(solution)/shard_map/pallas_call | solution.py:588
  58.6 1.0 %shard_map.104 = (bf16[128,2048]{1,0:T(8,128)(2,1)}, bf16[128,2048]{1,0:T(8,128)(2,1)}, f32[48,128]{1,0:T(8,128)}) custom-call(bf16[128,2048]{1,0:T(8,128)(2,1)S(1)} %get-tuple-element.9.produced_ref, bf16[128,2048]{1,0:T(8,128)(2,1)S(1)} %get-tuple-element.10.grads_ref, f32[48,128]{1,0:T(8,128)S(1)} %get-tuple-element.11.total_ref), custom_call_target="tpu_custom_call" | custom-call | tf_op jit(solution)/shard_map/pallas_call | solution.py:649

commit v3 on v2

--- a/solution.py
+++ b/solution.py
@@ -15,10 +15,11 @@
 PAIR = 2 * TOK
 SPAN = WINDOW + PAIR
 SLOTS = HEADS // 2
-OWN_AHEAD = 5
+OWN_AHEAD = 8
 AHEAD = 3
 PASS = 2
 DELAY = 4
+GATHER = 6
 EPSILON = 1e-06
 SCALE = HEAD_DIM**-0.5
 LOG2E = 1.4426950408889634
@@ -100,6 +101,7 @@
     up, down = c + 2 < n, c >= 2
     down2 = c >= 4
     level, levels = c // 2, n // 2
+    direct = levels <= 4
     stages = sum_stages(sizes)
     SWAP, COT, POS, PAIRS, RELAY, NEARG, FARG, OUT = range(8)
 
@@ -265,8 +267,9 @@
 
     def start_column(total):
         columns[level] = total
-        pl.when(up)(lambda: column_copy(level, 2).start())
-        pl.when(down)(lambda: column_copy(level, -2).start())
+        for k in range(1, levels if direct else 2):
+            pl.when(level + k < levels)(lambda: column_copy(level, 2 * k).start())
+            pl.when(level >= k)(lambda: column_copy(level, -2 * k).start())
 
     def pass_column(k):
         below, above = level - k, level + k
@@ -282,6 +285,14 @@
             pl.when(down)(lambda: column_copy(above, -2).start())
 
     def finish_column():
+        if direct:
+            for which in range(levels):
+                pl.when(level != which)(
+                    lambda: wait_bytes(columns.at[0], column_recv.at[which])
+                )
+        else:
+            for k in range(1, levels):
+                pass_column(k)
         total = columns[0]
         for which in range(1, levels):
             total = total + columns[which]
@@ -298,16 +309,6 @@
                 total_ref[pl.ds(m * HEADS + which * SLOTS, SLOTS), :] = halves[
                     which, pl.ds(m * SLOTS, SLOTS), :
                 ]
-
-    steps = [functools.partial(finish_sum, stage) for stage in range(len(stages))]
-    steps += [functools.partial(pass_column, k) for k in range(1, levels)]
-
-    def last_column():
-        pass_column(levels - 1)
-        finish_column()
-
-    steps[-1] = last_column
-    steps.append(finish_total)
 
     def each(action):
         @pl.loop(0, SLOTS)
@@ -414,9 +415,9 @@
         inverse = lax.rsqrt(jnp.mean(wide * wide, axis=-1, keepdims=True) + EPSILON)
         return wide * inverse, inverse
 
-    def probability(t, k, q, queries):
+    def weights(t, k, q, queries):
         w = jnp.exp2(dot(k, q, 1, 1) * (SCALE * LOG2E)) * masks[t, :, queries]
-        return w * (1.0 / jnp.sum(w, axis=0, keepdims=True))
+        return w, 1.0 / jnp.sum(w, axis=0, keepdims=True)
 
     sum_slot = digit_of(0) if stages else 0
 
@@ -427,7 +428,8 @@
         n_all, inverse = normed(x)
         k = (n_all * b).astype(BF16)
         q = (n_all[WINDOW:] * a).astype(BF16)
-        prob = probability(0, k, q, pl.ds(0, PAIR))
+        w, sum_inverse = weights(0, k, q, pl.ds(0, PAIR))
+        prob = w * sum_inverse
         p = prob.astype(BF16)
         ct = cot[j].astype(F32)
         d_mix = (ct * g).astype(BF16)
@@ -466,8 +468,8 @@
             rows = side if which == 0 else 1 - side
             mine = keys[1, j, part(OWN, rows)]
             q = (normed(mine)[0] * a).astype(BF16)
-            prob = probability(1, k, q, part(0, rows))
-            mix = dot(x, prob.astype(BF16), 0, 0).T
+            w, inverse = weights(1, k, q, part(0, rows))
+            mix = (dot(x, w.astype(BF16), 0, 0) * inverse).T
             produced[j, part(0, rows)] = (mine.astype(F32) + g * mix).astype(BF16)
             out_copy(0, j, which).start()
 
@@ -480,6 +482,8 @@
         pl.when(s + OWN_AHEAD < total)(lambda: pass_pair(s + OWN_AHEAD, side))
 
         pl.when(s + PASS < total)(lambda: relay(s + PASS))
+
+    def await_far(s):
         pl.when(down2)(lambda: wait_bytes(keys.at[0, 0, pl.ds(FAR, PAIR)], relay_recv.at[s]))
 
     def send_near(j):
@@ -492,6 +496,7 @@
 
     def first(j):
         feed(j, 2 * SLOTS)
+        await_far(j)
         wait_bytes(cot.at[0, pl.ds(0, TOK)], cot_recv.at[j])
         backward(j)
         pl.when(down2)(lambda: far_copy(j).start())
@@ -515,16 +520,20 @@
             out_copy(1, j, which).start()
 
     def last(j):
+        feed(j + SLOTS, 2 * SLOTS)
         pl.when(j < DELAY)(lambda: send_near(jnp.minimum(j + SLOTS - DELAY, SLOTS - 1)))
         send_dx(j)
-        for i, step in enumerate(steps[:SLOTS]):
-            pl.when(j == i)(step)
-        feed(j + SLOTS, 2 * SLOTS)
+        for stage in range(len(stages)):
+            pl.when(j == min(stage + 1, GATHER - 1))(lambda: finish_sum(stage))
+        if direct:
+            pl.when(j == GATHER)(finish_column)
+        await_far(j + SLOTS)
         forward(j)
 
     each(last)
-    for step in steps[SLOTS:]:
-        step()
+    if not direct:
+        finish_column()
+    finish_total()
 
     swapped = keys.at[:, :, pl.ds(0, TOK)]
     paired = keys.at[:, :, pl.ds(0, PAIR)]
@@ -535,12 +544,15 @@
     pl.when(up & down)(lambda: wait_bytes(paired, send_sem.at[RELAY]))
     pl.when(down)(lambda: wait_bytes(from_near, send_sem.at[NEARG]))
     pl.when(down2)(lambda: wait_bytes(from_far, send_sem.at[FARG]))
-    upward = jnp.where(up, level + 1, 0)
-    downward = jnp.where(down, levels - level, 0)
-
-    @pl.loop(0, upward + downward)
-    def _(_i):
-        wait_bytes(columns.at[0], pos_sem.at[4])
+    if direct:
+        wait_bytes(columns.at[pl.ds(0, levels - 1)], pos_sem.at[4])
+    else:
+        upward = jnp.where(up, level + 1, 0)
+        downward = jnp.where(down, levels - level, 0)
+
+        @pl.loop(0, upward + downward)
+        def _(_):
+            wait_bytes(columns.at[0], pos_sem.at[4])
 
     half_copy().wait_send()
     for stage, (_, _, factor) in enumerate(stages):

time: 60 us -> 56.5 us (0.942)
  Pallas kernels: 58.9 us -> 55.5 us
    pallas_call x1, Pallas kernels: 57.9 us -> 54.5 us  [local(): pl.pallas_call(functools.partial(kernel, sizes), out_shape=shapes, in_spe...]
where the time goes in v3:
time: 56.5 us; the launch traced here: 56.2 us
  Pallas kernels  55.5 us (98%)
  between operations  0.64 us (1%)
    pallas_call x1, Pallas kernels, local(): pl.pallas_call(functools.partial(kernel, sizes), out_shape=shapes, in_spe...  54.5 us

profile of v3, /device:TPU:17, one launch (start us, length us, event | category | flops | bytes accessed | tf_op | source)
XLA Modules:
  0.0 56.2 jit_solution(16872606032899360480)
XLA Ops:
  0.6 54.5 %shard_map.103 = (bf16[128,2048]{1,0:T(8,128)(2,1)S(1)}, bf16[128,2048]{1,0:T(8,128)(2,1)S(1)}, f32[48,128]{1,0:T(8,128)S(1)}) custom-call(bf16[128,2048]{1,0:T(8,128)(2,1)} %bitcast.10, s32[1,128]{1,0:T(1,128)} %bitcast.17, bf16[128,2048]{1,0:T(8,128)(2,1)} %bitcast.11, s32[1,128]{1,0:T(1,128)} %bitcast.18, bf16[128,2048]{1,0:T(8,128)(2,1)} %bitcast.12, ...), custom_call_target="tpu_custom_call" | custom-call | flops 3623878656 | bytes 2621440 | tf_op jit(solution)/shard_map/pallas_call | solution.py:600
  55.2 1.0 %shard_map.104 = (bf16[128,2048]{1,0:T(8,128)(2,1)}, bf16[128,2048]{1,0:T(8,128)(2,1)}, f32[48,128]{1,0:T(8,128)}) custom-call(bf16[128,2048]{1,0:T(8,128)(2,1)S(1)} %get-tuple-element.9.produced_ref, bf16[128,2048]{1,0:T(8,128)(2,1)S(1)} %get-tuple-element.10.grads_ref, f32[48,128]{1,0:T(8,128)S(1)} %get-tuple-element.11.total_ref), custom_call_target="tpu_custom_call" | custom-call | tf_op jit(solution)/shard_map/pallas_call | solution.py:661

commit v4 on v3

--- a/solution.py
+++ b/solution.py
@@ -16,7 +16,7 @@
 SPAN = WINDOW + PAIR
 SLOTS = HEADS // 2
 OWN_AHEAD = 8
-AHEAD = 3
+AHEAD = 4
 PASS = 2
 DELAY = 4
 GATHER = 6
@@ -27,17 +27,6 @@
 F32 = jnp.float32
 BF16 = jnp.bfloat16
 FAR, NEAR, OWN = 0, PAIR, 2 * PAIR
-
-
-def sum_stages(sizes):
-    stages = []
-    left, stride = sizes["dp"], 1
-    while left > 1:
-        factor = next(f for f in range(2, left + 1) if left % f == 0)
-        stages.append(("dp", stride, factor))
-        left //= factor
-        stride *= factor
-    return stages
 
 
 def dot(left, right, left_dim, right_dim):
@@ -74,8 +63,9 @@
     produced,
     dx,
     sums,
+    parts,
     columns,
-    halves,
+    shares,
     load_sem,
     small_sem,
     pos_sem,
@@ -87,9 +77,7 @@
     far_recv,
     out_recv,
     send_sem,
-    sum_send,
-    sum_recv,
-    column_recv,
+    gain_sem,
 ):
     n = sizes["ctx"]
     c = lax.axis_index("ctx")
@@ -102,7 +90,8 @@
     down2 = c >= 4
     level, levels = c // 2, n // 2
     direct = levels <= 4
-    stages = sum_stages(sizes)
+    replica, replicas = lax.axis_index("dp"), sizes["dp"]
+    per = SLOTS // replicas
     SWAP, COT, POS, PAIRS, RELAY, NEARG, FARG, OUT = range(8)
 
     def part(first, which):
@@ -211,104 +200,78 @@
             device,
         )
 
-    def digit_of(stage):
-        axis, stride, factor = stages[stage]
-        return lax.rem(lax.axis_index(axis) // stride, factor)
-
-    def sum_peer(stage, offset):
-        axis, stride, factor = stages[stage]
-        digit = digit_of(stage)
-        return {axis: lax.axis_index(axis) + (lax.rem(digit + offset, factor) - digit) * stride}
-
-    def sum_copy(stage, offset, sender):
-        return remote(
-            sums.at[stage, digit_of(stage)],
-            sums.at[stage, sender],
-            sum_send.at[stage, offset - 1],
-            sum_recv.at[stage, offset - 1],
-            sum_peer(stage, offset),
-        )
-
-    def half_copy():
-        return remote(
-            halves.at[side],
-            halves.at[side],
-            pos_sem.at[2],
-            pos_sem.at[3],
-            {"ctx": partner},
-        )
-
-    def start_sum(stage):
-        for offset in range(1, stages[stage][2]):
-            sum_copy(stage, offset, digit_of(stage)).start()
-
-    def finish_sum(stage):
-        factor = stages[stage][2]
-        for offset in range(1, factor):
-            sender = lax.rem(digit_of(stage) + factor - offset, factor)
-            sum_copy(stage, offset, sender).wait_recv()
-        total = sums[stage, 0]
-        for digit in range(1, factor):
-            total = total + sums[stage, digit]
-        if stage + 1 < len(stages):
-            sums[stage + 1, digit_of(stage + 1)] = total
-            start_sum(stage + 1)
-        else:
-            start_column(total)
-
-    def column_copy(which, step):
-        return remote(
-            columns.at[which],
-            columns.at[which],
-            pos_sem.at[4],
-            column_recv.at[which],
-            {"ctx": c + step},
-        )
-
-    def start_column(total):
-        columns[level] = total
-        for k in range(1, levels if direct else 2):
-            pl.when(level + k < levels)(lambda: column_copy(level, 2 * k).start())
-            pl.when(level >= k)(lambda: column_copy(level, -2 * k).start())
-
-    def pass_column(k):
-        below, above = level - k, level + k
-
-        @pl.when(below >= 0)
-        def _():
-            wait_bytes(columns.at[0], column_recv.at[below])
-            pl.when(up)(lambda: column_copy(below, 2).start())
-
-        @pl.when(above < levels)
-        def _():
-            wait_bytes(columns.at[0], column_recv.at[above])
-            pl.when(down)(lambda: column_copy(above, -2).start())
-
-    def finish_column():
+    def gain_copy(source, target, kind, device):
+        return remote(source, target, gain_sem.at[kind], gain_sem.at[kind + 1], device)
+
+    def start_sum():
+        parts[replica] = sums[replica]
+        for k in range(1, replicas):
+            peer = lax.rem(replica + k, replicas)
+            gain_copy(sums.at[peer], parts.at[replica], 0, {"dp": peer}).start()
+
+    def column_copy():
         if direct:
-            for which in range(levels):
-                pl.when(level != which)(
-                    lambda: wait_bytes(columns.at[0], column_recv.at[which])
-                )
-        else:
-            for k in range(1, levels):
-                pass_column(k)
+            return gain_copy(columns.at[level], columns.at[level], 2, {"ctx": side})
+        return gain_copy(columns.at[0], columns.at[1], 2, {"ctx": c - 2})
+
+    def start_column():
+        if replicas > 1:
+            wait_bytes(parts.at[pl.ds(0, replicas - 1)], gain_sem.at[1])
+        total = parts[0]
+        for which in range(1, replicas):
+            total = total + parts[which]
+        columns[level if direct else 0] = total
+        if direct:
+            pl.when(level > 0)(lambda: column_copy().start())
+
+    def spread(k):
+        gain_copy(shares.at[side * replicas + replica], shares.at[side * replicas + replica], 4, {"ctx": c + 2 * k}).start()
+
+    def top_column():
+        wait_bytes(columns.at[pl.ds(0, levels - 1)], gain_sem.at[3])
         total = columns[0]
         for which in range(1, levels):
             total = total + columns[which]
-        finish_half(total)
-
-    def finish_half(total):
-        halves[side] = total * (1.0 / TOK)
-        half_copy().start()
+        shares[side * replicas + replica] = total * (1.0 / TOK)
+        for k in range(1, levels):
+            spread(k)
+
+    def chain_column():
+        @pl.when(up)
+        def _():
+            wait_bytes(columns.at[0], gain_sem.at[3])
+            columns[0] = columns[0] + columns[1]
+
+        pl.when(down)(lambda: column_copy().start())
+
+        @pl.when(level == 0)
+        def _():
+            shares[side * replicas + replica] = columns[0] * (1.0 / TOK)
+
+    def start_share():
+        pl.when(level > 0)(lambda: wait_bytes(columns.at[0], gain_sem.at[5]))
+        if not direct:
+            pl.when(up)(lambda: spread(1))
+        for k in range(replicas):
+            peer = lax.rem(replica + k, replicas)
+            for which in ([partner] if k == 0 else [c, partner]):
+                gain_copy(
+                    shares.at[side * replicas + replica],
+                    shares.at[side * replicas + replica],
+                    6,
+                    {"ctx": which, "dp": peer},
+                ).start()
+
+    def wait_shares(kind):
+        wait_bytes(shares.at[pl.ds(0, 2 * replicas - 1)], gain_sem.at[kind])
 
     def finish_total():
-        half_copy().wait_recv()
+        wait_shares(7)
         for which in range(2):
-            for m in range(3):
-                total_ref[pl.ds(m * HEADS + which * SLOTS, SLOTS), :] = halves[
-                    which, pl.ds(m * SLOTS, SLOTS), :
-                ]
+            for chunk in range(replicas):
+                for m in range(3):
+                    first = m * HEADS + which * SLOTS + chunk * per
+                    total_ref[pl.ds(first, per), :] = shares[which * replicas + chunk, pl.ds(m * per, per), :]
 
     def each(action):
         @pl.loop(0, SLOTS)
@@ -331,10 +294,9 @@
     for condition, device in ((up, c + 2), (down, c - 2)):
         pl.when(condition)(lambda: greet({"ctx": device}))
         count = count + condition.astype(jnp.int32)
-    for stage, (_, _, factor) in enumerate(stages):
-        for offset in range(1, factor):
-            greet(sum_peer(stage, offset))
-            count += 1
+    for k in range(1, replicas):
+        greet({"dp": lax.rem(replica + k, replicas)})
+        count += 1
 
     each(lambda j: load(0, j).start())
     small = (
@@ -418,8 +380,6 @@
     def weights(t, k, q, queries):
         w = jnp.exp2(dot(k, q, 1, 1) * (SCALE * LOG2E)) * masks[t, :, queries]
         return w, 1.0 / jnp.sum(w, axis=0, keepdims=True)
-
-    sum_slot = digit_of(0) if stages else 0
 
     def backward(j):
         wide = lanes_of(side * SLOTS + j)
@@ -451,27 +411,41 @@
             d_value[:WINDOW] + through_norm(d_n[:WINDOW], n_all[:WINDOW], inverse[:WINDOW])
         ).astype(BF16)
         own[j] = d_value[WINDOW:] + through_norm(d_n_own, n_own, inverse[WINDOW:]) + ct
-        parts = (
+        gained = (
             jnp.sum(d_q * n_own, axis=0, keepdims=True) * SCALE,
             jnp.sum(d_k * n_all, axis=0, keepdims=True) * SCALE,
             jnp.sum(mixed * x, axis=0, keepdims=True),
         )
         for m in range(3):
-            sums[0, sum_slot, pl.ds(m * SLOTS + j, 1), :] = parts[m]
+            sums[j // per, pl.ds(m * per + lax.rem(j, per), 1), :] = gained[m]
 
     def forward(j):
         wide = lanes_of(side * SLOTS + j)
         a, b, g = (gains[pl.ds(m, 1), wide] for m in range(3))
-        x = keys[1, j]
-        k = (normed(x)[0] * b).astype(BF16)
-        for which in (1, 0):
-            rows = side if which == 0 else 1 - side
+
+        def attend(first, length, queries):
+            x = keys[1, j, pl.ds(first, length)]
+            k = (normed(x)[0] * b).astype(BF16)
+            found = []
+            for q, rows in queries:
+                scores = dot(k, q, 1, 1) * (SCALE * LOG2E)
+                w = jnp.exp2(scores) * masks[1, pl.ds(first, length), part(0, rows)]
+                found.append((jnp.sum(w, axis=0, keepdims=True), dot(x, w.astype(BF16), 0, 0)))
+            return found
+
+        queries = []
+        for rows in (1 - side, side):
             mine = keys[1, j, part(OWN, rows)]
-            q = (normed(mine)[0] * a).astype(BF16)
-            w, inverse = weights(1, k, q, part(0, rows))
-            mix = (dot(x, w.astype(BF16), 0, 0) * inverse).T
-            produced[j, part(0, rows)] = (mine.astype(F32) + g * mix).astype(BF16)
-            out_copy(0, j, which).start()
+            queries.append(((normed(mine)[0] * a).astype(BF16), rows))
+        close = attend(NEAR, SPAN - NEAR, queries)
+        await_far(j + SLOTS)
+        distant = attend(FAR, NEAR, queries)
+        for which, (_, rows) in enumerate(queries):
+            (sum_near, mix_near), (sum_far, mix_far) = close[which], distant[which]
+            mix = ((mix_near + mix_far) * (1.0 / (sum_near + sum_far))).T
+            mine = keys[1, j, part(OWN, rows)].astype(F32)
+            produced[j, part(0, rows)] = (mine + g * mix).astype(BF16)
+            out_copy(0, j, 1 - which).start()
 
     def feed(s, total):
         @pl.when(s + AHEAD < total)
@@ -504,10 +478,7 @@
         pl.when(j >= DELAY)(lambda: send_near(jnp.maximum(j - DELAY, 0)))
 
     each(first)
-    if stages:
-        start_sum(0)
-    else:
-        start_column(sums[0, 0])
+    start_sum()
 
     def send_dx(j):
         @pl.when(up)
@@ -523,16 +494,16 @@
         feed(j + SLOTS, 2 * SLOTS)
         pl.when(j < DELAY)(lambda: send_near(jnp.minimum(j + SLOTS - DELAY, SLOTS - 1)))
         send_dx(j)
-        for stage in range(len(stages)):
-            pl.when(j == min(stage + 1, GATHER - 1))(lambda: finish_sum(stage))
+        pl.when(j == 1)(start_column)
         if direct:
-            pl.when(j == GATHER)(finish_column)
-        await_far(j + SLOTS)
+            pl.when((j == GATHER) & (level == 0))(top_column)
+            pl.when(j == GATHER + 1)(start_share)
         forward(j)
 
     each(last)
     if not direct:
-        finish_column()
+        chain_column()
+        start_share()
     finish_total()
 
     swapped = keys.at[:, :, pl.ds(0, TOK)]
@@ -544,20 +515,14 @@
     pl.when(up & down)(lambda: wait_bytes(paired, send_sem.at[RELAY]))
     pl.when(down)(lambda: wait_bytes(from_near, send_sem.at[NEARG]))
     pl.when(down2)(lambda: wait_bytes(from_far, send_sem.at[FARG]))
+    if replicas > 1:
+        wait_bytes(sums.at[pl.ds(0, replicas - 1)], gain_sem.at[0])
+    pl.when(level > 0)(lambda: wait_bytes(columns.at[0], gain_sem.at[2]))
     if direct:
-        wait_bytes(columns.at[pl.ds(0, levels - 1)], pos_sem.at[4])
+        pl.when(level == 0)(lambda: wait_bytes(columns.at[pl.ds(0, levels - 1)], gain_sem.at[4]))
     else:
-        upward = jnp.where(up, level + 1, 0)
-        downward = jnp.where(down, levels - level, 0)
-
-        @pl.loop(0, upward + downward)
-        def _(_):
-            wait_bytes(columns.at[0], pos_sem.at[4])
-
-    half_copy().wait_send()
-    for stage, (_, _, factor) in enumerate(stages):
-        for offset in range(1, factor):
-            sum_copy(stage, offset, digit_of(stage)).wait_send()
+        pl.when(up)(lambda: wait_bytes(columns.at[0], gain_sem.at[4]))
+    wait_shares(6)
     for kind, (sent, target) in enumerate(((produced, next_ref), (dx, up_ref))):
         wait_bytes(sent, send_sem.at[OUT + kind])
         wait_bytes(target, out_recv.at[kind])
@@ -586,10 +551,8 @@
     output_gains,
     plan,
 ):
-    stages = sum_stages(sizes)
-    widest = max([factor for _, _, factor in stages] + [2])
-    depth = max(len(stages), 1)
-    levels = sizes["ctx"] // 2
+    replicas, levels = sizes["dp"], sizes["ctx"] // 2
+    part_shape = (3 * SLOTS // replicas, HEAD_DIM)
     anywhere = pl.BlockSpec(memory_space=pl.ANY)
     in_vmem = pl.BlockSpec(memory_space=pltpu.VMEM)
     shapes = (
@@ -617,12 +580,13 @@
             pltpu.VMEM((SLOTS, PAIR, HEAD_DIM), BF16),
             pltpu.VMEM((SLOTS, PAIR, HEAD_DIM), BF16),
             pltpu.VMEM((SLOTS, PAIR, HEAD_DIM), BF16),
-            pltpu.VMEM((depth, widest, 3 * SLOTS, HEAD_DIM), F32),
-            pltpu.VMEM((levels, 3 * SLOTS, HEAD_DIM), F32),
-            pltpu.VMEM((2, 3 * SLOTS, HEAD_DIM), F32),
+            pltpu.VMEM((replicas, *part_shape), F32),
+            pltpu.VMEM((replicas, *part_shape), F32),
+            pltpu.VMEM((levels, *part_shape), F32),
+            pltpu.VMEM((2 * replicas, *part_shape), F32),
             pltpu.SemaphoreType.DMA((3,)),
             pltpu.SemaphoreType.DMA((5,)),
-            pltpu.SemaphoreType.DMA((5,)),
+            pltpu.SemaphoreType.DMA((2,)),
             pltpu.SemaphoreType.DMA((2 * SLOTS,)),
             pltpu.SemaphoreType.DMA((SLOTS,)),
             pltpu.SemaphoreType.DMA((2 * SLOTS,)),
@@ -631,9 +595,7 @@
             pltpu.SemaphoreType.DMA((SLOTS,)),
             pltpu.SemaphoreType.DMA((2,)),
             pltpu.SemaphoreType.DMA((9,)),
-            pltpu.SemaphoreType.DMA((depth, widest - 1)),
-            pltpu.SemaphoreType.DMA((depth, widest - 1)),
-            pltpu.SemaphoreType.DMA((levels,)),
+            pltpu.SemaphoreType.DMA((8,)),
         ],
         compiler_params=pltpu.CompilerParams(
             collective_id=0, has_side_effects=True, vmem_limit_bytes=24 * 1024 * 1024

time: 56.5 us -> 54.9 us (0.972)
  Pallas kernels: 55.5 us -> 54.1 us
    pallas_call x1, Pallas kernels: 54.5 us -> 53.1 us  [local(): pl.pallas_call(functools.partial(kernel, sizes), out_shape=shapes, in_spe...]
where the time goes in v4:
time: 54.9 us; the launch traced here: 54.7 us
  Pallas kernels  54.1 us (99%)
  between operations  0.64 us (1%)
    pallas_call x1, Pallas kernels, local(): pl.pallas_call(functools.partial(kernel, sizes), out_shape=shapes, in_spe...  53.1 us

profile of v4, /device:TPU:17, one launch (start us, length us, event | category | flops | bytes accessed | tf_op | source)
XLA Modules:
  0.0 54.7 jit_solution(12930639910141656803)
XLA Ops:
  0.6 53.1 %shard_map.103 = (bf16[128,2048]{1,0:T(8,128)(2,1)S(1)}, bf16[128,2048]{1,0:T(8,128)(2,1)S(1)}, f32[48,128]{1,0:T(8,128)S(1)}) custom-call(bf16[128,2048]{1,0:T(8,128)(2,1)} %bitcast.10, s32[1,128]{1,0:T(1,128)} %bitcast.17, bf16[128,2048]{1,0:T(8,128)(2,1)} %bitcast.11, s32[1,128]{1,0:T(1,128)} %bitcast.18, bf16[128,2048]{1,0:T(8,128)(2,1)} %bitcast.12, ...), custom_call_target="tpu_custom_call" | custom-call | flops 3623878656 | bytes 2621440 | tf_op jit(solution)/shard_map/pallas_call | solution.py:563
  53.7 1.0 %shard_map.104 = (bf16[128,2048]{1,0:T(8,128)(2,1)}, bf16[128,2048]{1,0:T(8,128)(2,1)}, f32[48,128]{1,0:T(8,128)}) custom-call(bf16[128,2048]{1,0:T(8,128)(2,1)S(1)} %get-tuple-element.9.produced_ref, bf16[128,2048]{1,0:T(8,128)(2,1)S(1)} %get-tuple-element.10.grads_ref, f32[48,128]{1,0:T(8,128)S(1)} %get-tuple-element.11.total_ref), custom_call_target="tpu_custom_call" | custom-call | tf_op jit(solution)/shard_map/pallas_call | solution.py:623

commit v5 on v4

--- a/solution.py
+++ b/solution.py
@@ -18,8 +18,9 @@
 OWN_AHEAD = 8
 AHEAD = 4
 PASS = 2
-DELAY = 4
+DELAY = 5
 GATHER = 6
+GROUP = SLOTS // 2
 EPSILON = 1e-06
 SCALE = HEAD_DIM**-0.5
 LOG2E = 1.4426950408889634
@@ -127,7 +128,7 @@
             (sav_ref, sec_ref)[t].at[:, lanes_of((1 - side) * SLOTS + j)],
             keys.at[t, j, mine],
             send_sem.at[SWAP],
-            swap_recv.at[t * SLOTS + j],
+            swap_recv.at[SLOTS if t else j],
             {"ctx": partner},
         )
 
@@ -136,7 +137,7 @@
             cot_ref.at[:, lanes_of((1 - side) * SLOTS + j)],
             cot.at[j, part(0, side)],
             send_sem.at[COT],
-            cot_recv.at[j],
+            cot_recv.at[j // GROUP],
             {"ctx": partner},
         )
 
@@ -323,14 +324,23 @@
             pl.when(up)(lambda: relay_copy(s).start())
 
     def wait_swap(s):
-        wait_bytes(keys.at[0, 0, pl.ds(0, TOK)], swap_recv.at[s])
-
+        @pl.when(s < SLOTS)
+        def _():
+            wait_bytes(keys.at[0, 0, pl.ds(0, TOK)], swap_recv.at[jnp.minimum(s, SLOTS)])
+
+        pl.when(s == SLOTS)(
+            lambda: wait_bytes(keys.at[0, :, pl.ds(0, TOK)], swap_recv.at[SLOTS])
+        )
+
+    swap_copy(0, 0).start()
+    pass_pair(0, side)
+    pass_pair(1, side)
     for t in range(2):
         pos_copy(t).start()
 
     def first_swaps(j):
-        swap_copy(0, j).start()
-        pl.when(j < OWN_AHEAD)(lambda: pass_pair(j, side))
+        pl.when(j > 0)(lambda: swap_copy(0, j).start())
+        pl.when((j > 1) & (j < OWN_AHEAD))(lambda: pass_pair(j, side))
         cot_copy(j).start()
 
     each(first_swaps)
@@ -471,7 +481,9 @@
     def first(j):
         feed(j, 2 * SLOTS)
         await_far(j)
-        wait_bytes(cot.at[0, pl.ds(0, TOK)], cot_recv.at[j])
+        pl.when(lax.rem(j, GROUP) == 0)(
+            lambda: wait_bytes(cot.at[pl.ds(0, GROUP), pl.ds(0, TOK)], cot_recv.at[j // GROUP])
+        )
         backward(j)
         pl.when(down2)(lambda: far_copy(j).start())
         pl.when(down & jnp.logical_not(up))(lambda: near_copy(j).start())
@@ -496,8 +508,8 @@
         send_dx(j)
         pl.when(j == 1)(start_column)
         if direct:
-            pl.when((j == GATHER) & (level == 0))(top_column)
-            pl.when(j == GATHER + 1)(start_share)
+            pl.when((j == 4) & (level == 0))(top_column)
+            pl.when(j == 6)(start_share)
         forward(j)
 
     each(last)
@@ -587,8 +599,8 @@
             pltpu.SemaphoreType.DMA((3,)),
             pltpu.SemaphoreType.DMA((5,)),
             pltpu.SemaphoreType.DMA((2,)),
-            pltpu.SemaphoreType.DMA((2 * SLOTS,)),
-            pltpu.SemaphoreType.DMA((SLOTS,)),
+            pltpu.SemaphoreType.DMA((SLOTS + 1,)),
+            pltpu.SemaphoreType.DMA((2,)),
             pltpu.SemaphoreType.DMA((2 * SLOTS,)),
             pltpu.SemaphoreType.DMA((2 * SLOTS,)),
             pltpu.SemaphoreType.DMA((SLOTS,)),

time: 54.9 us -> 54.7 us (level)
  no operation moved by 1% of the time
where the time goes in v5:
time: 54.7 us; the launch traced here: 54.5 us
  Pallas kernels  53.9 us (99%)
  between operations  0.64 us (1%)
    pallas_call x1, Pallas kernels, local(): pl.pallas_call(functools.partial(kernel, sizes), out_shape=shapes, in_spe...  52.9 us

profile of v5, /device:TPU:17, one launch (start us, length us, event | category | flops | bytes accessed | tf_op | source)
XLA Modules:
  0.0 54.5 jit_solution(17982114431875973926)
XLA Ops:
  0.6 52.9 %shard_map.103 = (bf16[128,2048]{1,0:T(8,128)(2,1)S(1)}, bf16[128,2048]{1,0:T(8,128)(2,1)S(1)}, f32[48,128]{1,0:T(8,128)S(1)}) custom-call(bf16[128,2048]{1,0:T(8,128)(2,1)} %bitcast.10, s32[1,128]{1,0:T(1,128)} %bitcast.17, bf16[128,2048]{1,0:T(8,128)(2,1)} %bitcast.11, s32[1,128]{1,0:T(1,128)} %bitcast.18, bf16[128,2048]{1,0:T(8,128)(2,1)} %bitcast.12, ...), custom_call_target="tpu_custom_call" | custom-call | flops 3623878656 | bytes 2621440 | tf_op jit(solution)/shard_map/pallas_call | solution.py:575
  53.5 1.0 %shard_map.104 = (bf16[128,2048]{1,0:T(8,128)(2,1)}, bf16[128,2048]{1,0:T(8,128)(2,1)}, f32[48,128]{1,0:T(8,128)}) custom-call(bf16[128,2048]{1,0:T(8,128)(2,1)S(1)} %get-tuple-element.9.produced_ref, bf16[128,2048]{1,0:T(8,128)(2,1)S(1)} %get-tuple-element.10.grads_ref, f32[48,128]{1,0:T(8,128)S(1)} %get-tuple-element.11.total_ref), custom_call_target="tpu_custom_call" | custom-call | tf_op jit(solution)/shard_map/pallas_call | solution.py:635

commit v6 on v5

--- a/solution.py
+++ b/solution.py
@@ -175,7 +175,7 @@
             grads.at[j, pl.ds(NEAR, PAIR)],
             from_near.at[j],
             send_sem.at[NEARG],
-            near_recv.at[j],
+            near_recv.at[j // 2],
             {"ctx": c - 2},
         )
 
@@ -495,7 +495,9 @@
     def send_dx(j):
         @pl.when(up)
         def _():
-            near_copy(j).wait_recv()
+            pl.when(lax.rem(j, 2) == 0)(
+                lambda: wait_bytes(from_near.at[pl.ds(0, 2)], near_recv.at[j // 2])
+            )
             own[j] = own[j] + from_near[j].astype(F32)
 
         dx[j] = own[j].astype(BF16)
@@ -603,7 +605,7 @@
             pltpu.SemaphoreType.DMA((2,)),
             pltpu.SemaphoreType.DMA((2 * SLOTS,)),
             pltpu.SemaphoreType.DMA((2 * SLOTS,)),
-            pltpu.SemaphoreType.DMA((SLOTS,)),
+            pltpu.SemaphoreType.DMA((SLOTS // 2,)),
             pltpu.SemaphoreType.DMA((SLOTS,)),
             pltpu.SemaphoreType.DMA((2,)),
             pltpu.SemaphoreType.DMA((9,)),

time: 54.7 us -> 55.1 us (level)
  no operation moved by 1% of the time
where the time goes in v6:
time: 55.1 us; the launch traced here: 54.5 us
  Pallas kernels  53.9 us (98%)
  between operations  0.64 us (1%)
    pallas_call x1, Pallas kernels, local(): pl.pallas_call(functools.partial(kernel, sizes), out_shape=shapes, in_spe...  52.9 us

profile of v6, /device:TPU:17, one launch (start us, length us, event | category | flops | bytes accessed | tf_op | source)
XLA Modules:
  0.0 54.5 jit_solution(17380431854296059757)
XLA Ops:
  0.6 52.9 %shard_map.103 = (bf16[128,2048]{1,0:T(8,128)(2,1)S(1)}, bf16[128,2048]{1,0:T(8,128)(2,1)S(1)}, f32[48,128]{1,0:T(8,128)S(1)}) custom-call(bf16[128,2048]{1,0:T(8,128)(2,1)} %bitcast.10, s32[1,128]{1,0:T(1,128)} %bitcast.17, bf16[128,2048]{1,0:T(8,128)(2,1)} %bitcast.11, s32[1,128]{1,0:T(1,128)} %bitcast.18, bf16[128,2048]{1,0:T(8,128)(2,1)} %bitcast.12, ...), custom_call_target="tpu_custom_call" | custom-call | flops 3623878656 | bytes 2621440 | tf_op jit(solution)/shard_map/pallas_call | solution.py:577
  53.5 1.0 %shard_map.104 = (bf16[128,2048]{1,0:T(8,128)(2,1)}, bf16[128,2048]{1,0:T(8,128)(2,1)}, f32[48,128]{1,0:T(8,128)}) custom-call(bf16[128,2048]{1,0:T(8,128)(2,1)S(1)} %get-tuple-element.9.produced_ref, bf16[128,2048]{1,0:T(8,128)(2,1)S(1)} %get-tuple-element.10.grads_ref, f32[48,128]{1,0:T(8,128)S(1)} %get-tuple-element.11.total_ref), custom_call_target="tpu_custom_call" | custom-call | tf_op jit(solution)/shard_map/pallas_call | solution.py:637
